TPU v7x, 128 devices: a whole 4x4x4 slice. The times are simulated.
128 devices in a mesh: dom: 64 (over z, x, y), feat: 2 (over core).
Axes of the slice: x: 4, y: 4, z: 4, core: 2. Of those that a mesh axis runs over, the one named last changes fastest.
Arguments:
- features: bfloat16 [98304, 256], P('dom', 'feat'), may hold values from -6 to 6
- tile_weights: bfloat16 [40960, 128, 128], P('dom')
- tile_rows: int32 [40960], P('dom'), may hold values from 0 to 11, as said below
- tile_slots: int32 [40960], P('dom'), may hold values from 0 to 139, as said below
- send_blocks: int32 [64, 64, 2], P('dom'), may hold values from 0 to 11, as said below
- weight: bfloat16 [256, 256], replicated, may hold values from -0.375 to 0.375
- cotangent: bfloat16 [98304, 256], P(('dom', 'feat')), may hold values from -6 to 6
Outputs:
- hidden: bfloat16 [98304, 256], P(('dom', 'feat'))
- grad_features: bfloat16 [98304, 256], P('dom', 'feat')
- grad_weight: float32 [256, 256], P('feat')
Inputs may be any that keep to these rules, and one draw needn't show every extreme that they name: Within each partition tile_rows never falls; the first tile is in row block 0 and the last in row block 11. `tile_slots`: A partition never uses the slots of its own range 12 + d * 2 ...; from peer p it uses the first few of its 2 slots, and every used slot appears in some tile. Each partition reads exactly 2 blocks from the partition before it. `send_blocks`: local block indices of the owner, distinct within each owner and reader pair; every slot names a block, used or not.
All inputs are finite; a program needn't handle non-finite values.
Results may differ from a plain program's by a relative error of at most 0.0067.
Values may be sent and summed in bfloat16 or wider, within the bound.
A program may use at most 256 MiB of HBM per device.

v0:
```python
import jax
import jax.numpy as jnp
from jax import lax
from jax.sharding import PartitionSpec as P


def slope_of(pre):
    sigmoid_pre = jax.nn.sigmoid(pre)
    return sigmoid_pre * (1.0 + pre * (1.0 - sigmoid_pre))


def exact_dot(selector, values):
    return jnp.dot(
        selector, values, preferred_element_type=jnp.float32, precision=lax.Precision.HIGHEST
    )


def local(features, tile_weights, tile_rows, tile_slots, send_blocks, weight, cotangent):
    domains = lax.axis_size("dom")
    block_size = tile_weights.shape[1]
    tile_count = tile_weights.shape[0]
    rows_dev, half_width = features.shape
    blocks_dev = rows_dev // block_size
    own_blocks = features.reshape(blocks_dev, block_size, half_width)
    chosen = send_blocks[0].reshape(-1)
    block_ids = jnp.arange(blocks_dev, dtype=jnp.int32)
    chosen_match = chosen[:, None] == block_ids[None, :]
    outgoing = jnp.einsum(
        "cb,bjf->cjf",
        chosen_match.astype(jnp.bfloat16),
        own_blocks,
        preferred_element_type=jnp.float32,
    ).astype(jnp.bfloat16)
    outgoing = outgoing.reshape(send_blocks.shape[1], send_blocks.shape[2], block_size, half_width)
    arrived = lax.all_to_all(outgoing, "dom", split_axis=0, concat_axis=0, tiled=True)
    slot_total = blocks_dev + arrived.shape[0] * arrived.shape[1]
    buffer = jnp.concatenate([own_blocks, arrived.reshape(-1, block_size, half_width)], axis=0)
    slot_match = tile_slots[:, None] == jnp.arange(slot_total, dtype=jnp.int32)[None, :]
    picked = jnp.einsum(
        "ts,sjf->tjf", slot_match.astype(jnp.bfloat16), buffer, preferred_element_type=jnp.float32
    ).astype(jnp.bfloat16)
    products = jnp.einsum("tij,tjf->tif", tile_weights, picked, preferred_element_type=jnp.float32)
    row_match = block_ids[:, None] == tile_rows[None, :]
    summed = exact_dot(row_match.astype(jnp.float32), products.reshape(tile_count, -1))
    aggregated = summed.astype(jnp.bfloat16).reshape(rows_dev, half_width)
    factor = float(rows_dev * domains) ** (-0.5)
    full_rows = lax.all_to_all(aggregated, "feat", split_axis=0, concat_axis=1, tiled=True)
    pre = jnp.dot(full_rows, weight, preferred_element_type=jnp.float32)
    hidden = jax.nn.silu(pre).astype(jnp.bfloat16)
    grad_pre = (cotangent.astype(jnp.float32) * slope_of(pre)).astype(jnp.bfloat16)
    weight_term = jnp.dot(full_rows.T, grad_pre, preferred_element_type=jnp.float32)
    weight_part = lax.psum_scatter(weight_term, "feat", scatter_dimension=0, tiled=True)
    grad_full = jnp.dot(grad_pre, weight.T, preferred_element_type=jnp.float32).astype(jnp.bfloat16)
    grad_cols = lax.all_to_all(grad_full, "feat", split_axis=1, concat_axis=0, tiled=True)
    grad_weight = lax.psum(weight_part, "dom") * factor
    col_blocks = grad_cols.reshape(blocks_dev, block_size, half_width)
    gathered = jnp.einsum(
        "rt,rjf->tjf",
        row_match.astype(jnp.bfloat16),
        col_blocks,
        preferred_element_type=jnp.float32,
    ).astype(jnp.bfloat16)
    back_terms = jnp.einsum(
        "tji,tjf->tif", tile_weights, gathered, preferred_element_type=jnp.float32
    )
    per_slot = exact_dot(slot_match.T.astype(jnp.float32), back_terms.reshape(tile_count, -1))
    per_slot = per_slot.reshape(slot_total, block_size, half_width)
    leaving = per_slot[blocks_dev:].astype(jnp.bfloat16).reshape(arrived.shape)
    returned = lax.all_to_all(leaving, "dom", split_axis=0, concat_axis=0, tiled=True)
    returned_flat = returned.reshape(-1, block_size * half_width).astype(jnp.float32)
    incoming = exact_dot(chosen_match.T.astype(jnp.float32), returned_flat).reshape(
        blocks_dev, block_size, half_width
    )
    grad_features = (
        (per_slot[:blocks_dev] + incoming).astype(jnp.bfloat16).reshape(rows_dev, half_width)
    )
    return (hidden, grad_features, grad_weight)


def solution(mesh):
    placed = (
        P("dom", "feat"),
        P("dom", None, None),
        P("dom"),
        P("dom"),
        P("dom", None, None),
        P(),
        P(("dom", "feat"), None),
    )
    return jax.shard_map(
        local,
        mesh=mesh,
        in_specs=placed,
        out_specs=(P(("dom", "feat"), None), P("dom", "feat"), P("feat", None)),
        check_vma=False,
    )
```

profile of v0, /device:TPU:2, one launch (start us, length us, event | category | flops | bytes accessed | tf_op | source)
XLA Modules:
  0.0 532.2 jit_solution(12921760855125089515)
XLA Ops:
  8.2 2.3 convolution_convert_fusion.3
  10.5 6.6 %copy.55 = bf16[64,2,128,128]{3,1,2,0:T(2,128)(2,1)} copy(bf16[64,2,128,128]{3,1,0,2:T(2,128)(2,1)S(1)} %bitcast.59) | data formatting | bytes 8388608 | tf_op jit(solution)/shard_map/reshape | solution.py:34
  17.1 12.2 %all-to-all-start = ((bf16[64,2,128,128]{3,1,2,0:T(2,128)(2,1)}), bf16[64,2,128,128]{3,1,2,0:T(2,128)(2,1)}, u32[]{:S(2)}, u32[]{:S(2)}) async-start(bf16[64,2,128,128]{3,1,2,0:T(2,128)(2,1)} %copy.55), calls=%async_computation | async-start | bytes 8388608 | tf_op jit(solution)/shard_map/all_to_all | solution.py:35
  29.6 52.5 %all-to-all-done = bf16[64,2,128,128]{3,1,2,0:T(2,128)(2,1)} async-done(((bf16[64,2,128,128]{3,1,2,0:T(2,128)(2,1)}), bf16[64,2,128,128]{3,1,2,0:T(2,128)(2,1)}, u32[]{:S(2)}, u32[]{:S(2)}) %all-to-all-start) | async-done | bytes 4194336 | tf_op jit(solution)/shard_map/all_to_all | solution.py:35
  82.0 6.9 %copy.56 = bf16[64,2,128,128]{3,1,0,2:T(2,128)(2,1)S(1)} copy(bf16[64,2,128,128]{3,1,2,0:T(2,128)(2,1)} %all-to-all-done) | data formatting | bytes 8388608 | tf_op jit(solution)/shard_map/all_to_all | solution.py:35
  89.0 10.0 %convolution_convert_fusion.1 = bf16[640,128,128]{2,0,1:T(8,128)(2,1)} fusion(bf16[128,128,128]{2,0,1:T(8,128)(2,1)S(1)} %bitcast.60, bf16[12,128,128]{2,0,1:T(8,128)(2,1)S(1)} %copy.57, s32[640]{0:T(1024)S(1)} %copy-done.4), kind=kOutput, calls=%fused_computation.7 | convolution fusion | flops 2955763200 | bytes 25561600 | tf_op jit(solution)/shard_map/ts,sjf->tjf/dot_general | solution.py:39
  99.0 36.5 %fusion.4 = f32[640,128,128]{1,2,0:T(8,128)} fusion(bf16[640,128,128]{2,1,0:T(8,128)(2,1)} %param.8, bf16[640,128,128]{2,0,1:T(8,128)(2,1)} %convolution_convert_fusion.1), kind=kOutput, calls=%fused_computation.5 | convolution fusion | flops 2684354560 | bytes 83886080 | tf_op jit(solution)/shard_map/tij,tjf->tif/dot_general | solution.py:42
  135.5 44.0 %copy.59 = f32[640,128,128]{0,2,1:T(8,128)} copy(f32[640,128,128]{1,2,0:T(8,128)} %fusion.4) | data formatting | bytes 83886080 | tf_op jit(solution)/shard_map/tij,tjf->tif/dot_general | solution.py:42
  179.5 22.8 %convolution_convert_fusion = bf16[12,16384]{1,0:T(8,128)(2,1)S(1)} fusion(f32[640,16384]{0,1:T(8,128)} %bitcast.53, s32[640]{0:T(1024)S(1)} %copy-done.3), kind=kOutput, calls=%fused_computation.4 | convolution fusion | flops 1510153728 | bytes 42338816 | tf_op jit(solution)/shard_map/dot_general | solution.py:13
  202.9 4.2 all_to_all.45
  208.9 4.0 all_to_all.46
  213.0 9.9 %convolution_convert_fusion.2 = bf16[640,128,128]{2,0,1:T(8,128)(2,1)} fusion(bf16[12,128,128]{2,1,0:T(8,128)(2,1)S(1)} %bitcast.61, s32[640]{0:T(1024)S(1)} %copy-done.3), kind=kOutput, calls=%fused_computation.8 | convolution fusion | flops 262151680 | bytes 21367296 | tf_op jit(solution)/shard_map/rt,rjf->tjf/dot_general | solution.py:57
  222.9 35.9 %fusion.7 = f32[640,128,128]{1,2,0:T(8,128)} fusion(bf16[640,128,128]{2,1,0:T(8,128)(2,1)} %param.8, bf16[640,128,128]{2,0,1:T(8,128)(2,1)} %convolution_convert_fusion.2), kind=kOutput, calls=%fused_computation.6 | convolution fusion | flops 2684354560 | bytes 83886080 | tf_op jit(solution)/shard_map/tji,tjf->tif/dot_general | solution.py:63
  258.7 44.0 %copy.64 = f32[640,128,128]{0,2,1:T(8,128)} copy(f32[640,128,128]{1,2,0:T(8,128)} %fusion.7) | data formatting | bytes 83886080 | tf_op jit(solution)/shard_map/tji,tjf->tif/dot_general | solution.py:63
  302.8 25.9 %fusion.16 = f32[140,16384]{1,0:T(8,128)} fusion(f32[640,16384]{0,1:T(8,128)} %bitcast.54, s32[640]{0:T(1024)S(1)} %copy-done.4), kind=kOutput, calls=%fused_computation.24 | convolution fusion | flops 17616166912 | bytes 51120640 | tf_op jit(solution)/shard_map/dot_general | solution.py:13
  328.6 4.7 fusion.13
  333.4 3.2 copy.68
  336.6 8.1 %all-to-all-start.3 = ((bf16[64,2,128,128]{3,2,1,0:T(8,128)(2,1)}), bf16[64,2,128,128]{3,2,1,0:T(8,128)(2,1)}, u32[]{:S(2)}, u32[]{:S(2)}) async-start(bf16[64,2,128,128]{3,2,1,0:T(8,128)(2,1)} %bitcast.56), calls=%async_computation.3 | async-start | bytes 8388608 | tf_op jit(solution)/shard_map/all_to_all | solution.py:69
  345.8 14.3 %reduce-scatter.2.cloned.1.call-done = f32[128,256]{1,0:T(8,128)} async-done(((f32[256,256]{1,0:T(8,128)}), f32[128,256]{1,0:T(8,128)}) %reduce-scatter.2.cloned.1.call-update) | async-done | bytes 131088 | tf_op jit(solution)/shard_map/reduce_scatter | solution.py:52
  360.3 144.6 %all-reduce.2.cloned.1.call-done = f32[128,256]{1,0:T(8,128)} async-done(((f32[128,256]{1,0:T(8,128)}), f32[128,256]{1,0:T(8,128)}) %all-reduce.2.cloned.1.call-update) | async-done | bytes 131088 | tf_op jit(solution)/shard_map/psum | solution.py:55
  504.9 1.6 broadcast_multiply_fusion
  506.5 7.7 %copy.84 = bf16[16,8,128,128]{3,1,2,0:T(8,128)(2,1)} copy(bf16[16,8,128,128]{3,2,1,0:T(8,128)(2,1)} %bitcast.28) | data formatting | bytes 8388608
  514.2 6.4 %copy.65 = bf16[128,16384]{0,1:T(8,128)(2,1)} copy(bf16[128,16384]{1,0:T(8,128)(2,1)} %bitcast.58) | data formatting | bytes 8388608 | tf_op jit(solution)/shard_map/reshape | solution.py:70
  520.6 3.4 fusion.26
  (34 shorter events, 6.0 us)
Async XLA Ops:
  7.2 199.9 %copy-start = (bf16[256,256]{1,0:T(8,128)(2,1)S(1)}, bf16[256,256]{1,0:T(8,128)(2,1)}, u32[]{:S(2)}) copy-start(bf16[256,256]{1,0:T(8,128)(2,1)} %param.12) | copy-start | bytes 393220
  7.2 22.1 %copy-start.2 = (bf16[1536,128]{1,0:T(8,128)(2,1)S(1)}, bf16[1536,128]{1,0:T(8,128)(2,1)}, u32[]{:S(2)}) copy-start(bf16[1536,128]{1,0:T(8,128)(2,1)} %param.7) | copy-start | bytes 1179652
  7.2 81.8 %copy-start.4 = (s32[640]{0:T(1024)S(1)}, s32[640]{0:T(1024)}, u32[]{:S(2)}) copy-start(s32[640]{0:T(1024)} %param.10) | copy-start | bytes 7684
  8.2 8.9 %copy-start.5 = (s32[128]{0:T(128)}, s32[128]{0:T(128)S(1)}, u32[]{:S(2)}) copy-start(s32[128]{0:T(128)S(1)} %eq.47) | copy-start | bytes 1540
  17.1 65.0 %all-to-all-start = ((bf16[64,2,128,128]{3,1,2,0:T(2,128)(2,1)}), bf16[64,2,128,128]{3,1,2,0:T(2,128)(2,1)}, u32[]{:S(2)}, u32[]{:S(2)}) async-start(bf16[64,2,128,128]{3,1,2,0:T(2,128)(2,1)} %copy.55), calls=%async_computation | async-start | bytes 8388608 | tf_op jit(solution)/shard_map/all_to_all | solution.py:35
  135.5 44.0 %copy-start.3 = (s32[640]{0:T(1024)S(1)}, s32[640]{0:T(1024)}, u32[]{:S(2)}) copy-start(s32[640]{0:T(1024)} %param.9) | copy-start | bytes 7684
  179.5 27.6 %copy-start.7 = (bf16[768,256]{1,0:T(8,128)(2,1)S(1)}, bf16[768,256]{1,0:T(8,128)(2,1)}, u32[]{:S(2)}) copy-start(bf16[768,256]{1,0:T(8,128)(2,1)} %param.13) | copy-start | bytes 1179652
  328.6 31.4 %slice-start = ((f32[140,16384]{1,0:T(8,128)}), f32[12,16384]{1,0:T(8,128)S(1)}, s32[]{:S(2)}) async-start(f32[140,16384]{1,0:T(8,128)} %fusion.16), calls=%async_computation.7 | async-start | bytes 2097152 | tf_op jit(solution)/shard_map/slice | solution.py:75
  333.3 187.3 %copy-start.6 = (s32[128]{0:T(128)S(1)}, s32[128]{0:T(128)}, u32[]{:S(2)}) copy-start(s32[128]{0:T(128)} %copy-done.5) | copy-start | bytes 1540
  333.3 191.8 %copy-start.1 = (bf16[256,256]{1,0:T(8,128)(2,1)S(1)}, bf16[256,256]{1,0:T(8,128)(2,1)}, u32[]{:S(2)}) copy-start(bf16[256,256]{1,0:T(8,128)(2,1)} %param.12) | copy-start | bytes 393220
  336.6 170.0 %all-to-all-start.3 = ((bf16[64,2,128,128]{3,2,1,0:T(8,128)(2,1)}), bf16[64,2,128,128]{3,2,1,0:T(8,128)(2,1)}, u32[]{:S(2)}, u32[]{:S(2)}) async-start(bf16[64,2,128,128]{3,2,1,0:T(8,128)(2,1)} %bitcast.56), calls=%async_computation.3 | async-start | bytes 8388608 | tf_op jit(solution)/shard_map/all_to_all | solution.py:69
  344.7 15.4 %reduce-scatter.2.cloned.1.call-start = ((), (), s32[]{:S(2)}) async-start(), calls=%async_computation.5 | async-start | bytes 393216 | tf_op jit(solution)/shard_map/reduce_scatter | solution.py:52
  345.7 159.2 %all-reduce.2.cloned.1.call-start = ((), (), s32[]{:S(2)}) async-start(), calls=%async_computation.6 | async-start | bytes 262144 | tf_op jit(solution)/shard_map/psum | solution.py:55
Sparse Core Ops, SparseCore 0:
  348.4 11.5 reduce-scatter.1
  365.5 139.4 all-reduce.1
where the time goes:
time: 539 us; the launch traced here: 532 us
  waiting for transfers between devices  211 us (39%)
  matrix products  149 us (28%)
  local copies, waits for them, and re-layouts  126 us (23%)
  starting transfers between devices  20.4 us (4%)
  between operations  14.4 us (3%)
  blocking collectives  8.26 us (2%)
    psum x1, waiting for transfers between devices, local(): grad_weight = lax.psum(weight_part, 'dom') * factor  145 us
    all_to_all x1, waiting for transfers between devices, local(): lax.all_to_all(outgoing, 'dom', split_axis=0, concat_axis=0, tiled=True)  52.5 us
    dot_general x3, matrix products, exact_dot(): jnp.dot(selector, values, preferred_element_type=jnp.float32, precision=l...  52.1 us
    dot_general x1, local copies, waits for them, and re-layouts, local(): jnp.einsum('tij,tjf->tif', tile_weights, picked, preferred_element_type=j...  44 us
    dot_general x1, local copies, waits for them, and re-layouts, local(): jnp.einsum('tji,tjf->tif', tile_weights, gathered, preferred_element_type...  44 us
    dot_general x1, matrix products, local(): jnp.einsum('tij,tjf->tif', tile_weights, picked, preferred_element_type=j...  36.5 us
    dot_general x1, matrix products, local(): jnp.einsum('tji,tjf->tif', tile_weights, gathered, preferred_element_type...  35.9 us
    unnamed x21, local copies, waits for them, and re-layouts  16.7 us
  transfers between devices with their start and end apart: 4, of which 3 were waited for; matrix products, arithmetic and copies ran while one was open for 1% of the time, Pallas kernels for 0%

commit v1 on v0

v1 whole, which is shorter than its diff:
```python
import functools

import jax
import jax.numpy as jnp
from jax import lax
from jax.experimental import pallas as pl
from jax.experimental.pallas import tpu as pltpu
from jax.sharding import PartitionSpec as P

MESH = pl.DeviceIdType.MESH
F32, BF16, I32 = jnp.float32, jnp.bfloat16, jnp.int32

BLK = 128
NB = 12
TILES = 640
SIDE = 4
NVAR = 3
ROWS = (48, 48, 32)
FIRST = (0, 48, 96)

FC, BC = 8, 2
FU = 92
BU = 390
FCH, BCH = 6, 7

X_OWN, X_HOP, X_END, X_SIZE = 1, 16, 144, 240
Y_ONE, Y_TWO, Y_SIZE = 128, 224, 320
RUN_ZERO = BU
OFFS = (1, 3, 2)


def body(
    feats, tiles_hbm, rows_ref, slots_ref, tab_ref, tab_sm, weight, cot,
    hidden, grad_out, gw_out,
    w, x0, x1, x2, y0, y1, y2, ag0, ag1, ag2, v0, v1, v2, rr0, rr1, rr2,
    runs, tabs, tabs_sm, flist, flist_sm, blist, blist_sm, ends, ends_sm, rlist, rlist_sm,
    full, send_a, gt, send_g, wt, wt_in, gw0, gw1, gw2, gw3,
    w_sem, sm_sem, feat_s, feat_r, tab_s, tab_r,
    s1_s, s1_r, s2_s, s2_r, s3_s, s3_r, b3_s, b3_r, b2_s, b2_r, b1_s, b1_r, gw_s, gw_r,
):
    x, y, ag, vin, rr = (x0, x1, x2), (y0, y1, y2), (ag0, ag1, ag2), (v0, v1, v2), (rr0, rr1, rr2)
    dom, feat = lax.axis_index("dom"), lax.axis_index("feat")
    cz, cx, cy = lax.div(dom, 16), lax.rem(lax.div(dom, 4), 4), lax.rem(dom, 4)

    def moved(axis_is_z, axis_is_x, off):
        z = lax.rem(cz + off, 4) * 16 + cx * 4 + cy
        xx = cz * 16 + lax.rem(cx + off, 4) * 4 + cy
        yy = cz * 16 + cx * 4 + lax.rem(cy + off, 4)
        return jnp.where(axis_is_z, z, jnp.where(axis_is_x, xx, yy))

    turn = [lax.rem(v + feat, 3) for v in range(NVAR)]

    def role(v, which):
        axis = lax.rem(turn[v] + which, 3)
        return axis == 0, axis == 1

    def peer(v, which, off):
        return (moved(*role(v, which), off), feat)

    def reader(v, db, dc):
        z, xx, yy = (lax.rem(c + d, 4) for c, d in ((cz, 0), (cx, 0), (cy, 0)))
        t = turn[v]
        z = lax.rem(cz + jnp.where(t == 1, dc, jnp.where(t == 2, db, 0)), 4)
        xx = lax.rem(cx + jnp.where(t == 0, db, jnp.where(t == 2, dc, 0)), 4)
        yy = lax.rem(cy + jnp.where(t == 0, dc, jnp.where(t == 1, db, 0)), 4)
        return z * 16 + xx * 4 + yy

    started = []

    def send(src, dst, ssem, rsem, device):
        cp = pltpu.make_async_remote_copy(
            src_ref=src, dst_ref=dst, send_sem=ssem, recv_sem=rsem, device_id=device, device_id_type=MESH
        )
        cp.start()
        started.append(cp)
        return cp

    other = (dom, 1 - feat)

    barrier = pltpu.get_barrier_semaphore()
    for axis in range(3):
        for off in (1, 2, 3):
            pl.semaphore_signal(
                barrier, inc=1, device_id=(moved(axis == 0, axis == 1, off), feat), device_id_type=MESH
            )
    pl.semaphore_signal(barrier, inc=1, device_id=other, device_id_type=MESH)
    pl.semaphore_wait(barrier, 10)

    tab_cp, s1, s2, s3 = {}, {}, {}, {}
    for v in range(NVAR):
        for off in OFFS:
            i = v * 4 + off
            tab_cp[v, off] = send(tab_ref, tabs.at[v * 4 + (4 - off)], tab_s.at[i], tab_r.at[i], peer(v, 0, off))
    for off in OFFS:
        for v in range(NVAR):
            i = v * 4 + off
            s1[v, off] = send(
                feats.at[:, pl.ds(FIRST[v], ROWS[v])], ag[v].at[pl.ds((4 - off) * NB, NB)],
                s1_s.at[i], s1_r.at[i], peer(v, 0, off),
            )
    w_cp = pltpu.make_async_copy(tiles_hbm, w, w_sem.at[0])
    w_cp.start()

    for v in range(NVAR):
        chunk = pl.ds(FIRST[v], ROWS[v])
        x[v][0] = jnp.zeros((ROWS[v], BLK), BF16)
        for j in range(NB):
            block = feats[j, chunk]
            x[v][X_OWN + j] = block
            ag[v][j] = block
        tabs[v * 4] = tab_ref[...]

    lane = lax.broadcasted_iota(I32, (BLK, BLK), 1)
    sub = lax.broadcasted_iota(I32, (BLK, BLK), 0)
    ones = jnp.ones((BLK, BLK), I32)

    def column(row):
        return jnp.transpose(ones * row)

    def hits(mask):
        return jnp.where(mask, 1, 0)

    chunks = range(TILES // BLK)

    row_r = [rows_ref[pl.ds(c, 1), :] for c in chunks]
    slot_r = [slots_ref[pl.ds(c, 1), :] for c in chunks]
    row_c = [column(r) for r in row_r]
    lane1 = lane[0:1]
    row_count = sum(jnp.sum(hits(r == lane), axis=0, keepdims=True) for r in row_c)
    row_units = lax.shift_right_logical(row_count + (FC - 1), FC.bit_length() - 1)
    row_units_c, row_count_c = column(row_units), column(row_count)
    row_first = jnp.sum(jnp.where(sub < lane, row_units_c, 0), axis=0, keepdims=True)
    row_begin = jnp.sum(jnp.where(sub < lane, row_count_c, 0), axis=0, keepdims=True)
    row_last = jnp.where(row_count > 0, row_first + row_units - 1, RUN_ZERO)
    ends[pl.ds(2, 1), :] = row_last

    def digits(block):
        pz, px, py = lax.shift_right_logical(block, 4), lax.shift_right_logical(block, 2) & 3, block & 3
        return (pz - cz) & 3, (px - cx) & 3, (py - cy) & 3

    def roles(v, rel):
        rz, rx, ry = rel
        t = turn[v]
        first = jnp.where(t == 0, rz, jnp.where(t == 1, rx, ry))
        second = jnp.where(t == 0, rx, jnp.where(t == 1, ry, rz))
        third = jnp.where(t == 0, ry, jnp.where(t == 1, rz, rx))
        return first, second, third

    def x_entry(v, slot):
        far = jnp.maximum(slot - NB, 0)
        k = far & 1
        d, b, g = roles(v, digits(lax.shift_right_logical(far, 1)))
        near = X_HOP + ((b * 4) * 4 + d) * 2 + k
        end = X_END + (((g - 1) * 4 + b) * 4 + d) * 2 + k
        return jnp.where(slot < NB, X_OWN + slot, jnp.where(g == 0, near, end))

    place, tile_c = [], []
    for c in chunks:
        offset = jnp.sum(jnp.where(row_c[c] == lane, FC * row_first - row_begin, 0), axis=1, keepdims=True)
        tile_c.append(sub + c * BLK)
        place.append(offset + tile_c[c])
    for v in range(NVAR):
        entry_c = [column(x_entry(v, s)) for s in slot_r]
        for q in range(FCH):
            at = lane + q * BLK
            found = sum(
                jnp.sum(jnp.where(place[c] == at, entry_c[c], 0), axis=0, keepdims=True) for c in chunks
            )
            flist[pl.ds((v + 1) * 8 + q, 1), :] = found
    for q in range(FCH):
        at = lane + q * BLK
        found = sum(
            jnp.sum(jnp.where(place[c] == at, tile_c[c], 0), axis=0, keepdims=True) for c in chunks
        )
        flist[pl.ds(q, 1), :] = found
        starts = sum(
            jnp.sum(
                jnp.where(
                    (place[c] == at)
                    & (tile_c[c] == jnp.sum(jnp.where(row_c[c] == lane, row_begin, 0), axis=1, keepdims=True)),
                    1, 0,
                ),
                axis=0, keepdims=True,
            )
            for c in chunks
        )
        flist[pl.ds(32 + q, 1), :] = starts

    for v in range(NVAR):
        for off in OFFS:
            tab_cp[v, off].wait_recv()
    tabs_cp = pltpu.make_async_copy(tabs, tabs_sm, sm_sem.at[0])
    tabs_cp.start()
    tabs_cp.wait()

    def pack(v, db, dc, dst, base):
        at = reader(v, db, dc) * 2
        for d in range(4):
            for k in range(2):
                j = tabs_sm[v * 4 + d, 0, at + k]
                dst[base + d * 2 + k] = ag[v][d * NB + j]

    def pass_on(v, b, dc):
        i = (v * 4 + b) * 4 + dc
        s3[v, b, dc] = send(
            x[v].at[pl.ds(X_HOP + (b * 4 + dc) * 8, 8)],
            x[v].at[pl.ds(X_END + ((4 - dc - 1) * 4 + b) * 8, 8)],
            s3_s.at[i], s3_r.at[i], peer(v, 2, dc),
        )

    for v in range(NVAR):
        for off in OFFS:
            s1[v, off].wait_recv()
        for dc in (1, 3, 2, 0):
            pack(v, 0, dc, x[v], X_HOP + dc * 8)
            if dc:
                pass_on(v, 0, dc)
            for db in OFFS:
                base = (db * 4 + dc) * 8
                pack(v, db, dc, y[v], base)
                i = (v * 4 + db) * 4 + dc
                s2[v, db, dc] = send(
                    y[v].at[pl.ds(base, 8)], x[v].at[pl.ds(X_HOP + ((4 - db) * 4 + dc) * 8, 8)],
                    s2_s.at[i], s2_r.at[i], peer(v, 1, db),
                )

    slot_c = [column(s) for s in slot_r]
    counts = [sum(jnp.sum(hits(s == lane + h * BLK), axis=0, keepdims=True) for s in slot_c) for h in range(2)]
    units = [lax.shift_right_logical(n + (BC - 1), BC.bit_length() - 1) for n in counts]
    units_c = [column(u) for u in units]
    firsts = [
        jnp.sum(jnp.where(sub < lane, units_c[0], 0), axis=0, keepdims=True),
        jnp.sum(jnp.where(sub < lane, units_c[1], 0) + units_c[0], axis=0, keepdims=True),
    ]
    for h in range(2):
        last = jnp.where(counts[h] > 0, firsts[h] + units[h] - 1, RUN_ZERO)
        ends[pl.ds(h, 1), :] = last
    order, place = [], []
    for c in chunks:
        before = sum(hits((slot_c[c] == slot_r[e]) & (lane + e * BLK < tile_c[c])) for e in chunks)
        order.append(jnp.sum(before, axis=1, keepdims=True))
        begin = jnp.sum(
            sum(jnp.where(slot_c[c] == lane + h * BLK, firsts[h], 0) for h in range(2)),
            axis=1, keepdims=True,
        )
        place.append(ones * (BC * begin + order[c]))
    start_c = [hits(o == 0) * ones for o in order]
    row_next = [r + 1 for r in row_c]
    for q in range(BCH):
        at = lane + q * BLK
        for base, what in ((0, tile_c), (8, row_next), (16, start_c)):
            found = sum(jnp.sum(jnp.where(place[c] == at, what[c], 0), axis=0, keepdims=True) for c in chunks)
            blist[pl.ds(base + q, 1), :] = found

    index1 = lax.broadcasted_iota(I32, (1, BLK), 1)
    for v in range(NVAR):
        k = index1 & 1
        d, b, g = roles(v, digits(lax.shift_right_logical(index1, 1)))
        own = Y_TWO + ((b - 1) * 4 + g) * 8 + k
        loc = jnp.where(b > 0, own, jnp.where(g > 0, Y_ONE + (g - 1) * 32 + k, k))
        loc_c = column(loc)
        for o in range(4):
            block = jnp.where(d == 0, tabs[v * 4 + o], 64)
            key = block * 128 + lane1
            block_c, key_c = column(block), column(key)
            rank = jnp.sum(hits(key_c < key), axis=0, keepdims=True)
            begin = jnp.sum(hits(block_c < block), axis=0, keepdims=True)
            rank_c, begin_c = column(rank), column(begin)
            value = loc_c + o * 2 + 512 * hits(rank_c == begin_c)
            found = jnp.sum(jnp.where(rank_c == lane, value, 0), axis=0, keepdims=True)
            upto = jnp.sum(hits(block_c <= lane), axis=0, keepdims=True)
            count = jnp.sum(hits(block_c == lane), axis=0, keepdims=True)
            rlist[pl.ds((v * 4 + o) * 2, 1), :] = found
            rlist[pl.ds((v * 4 + o) * 2 + 1, 1), :] = jnp.where(count > 0, upto - 1, 32)

    to_sm = [
        pltpu.make_async_copy(a, b, sm_sem.at[1 + i])
        for i, (a, b) in enumerate(((flist, flist_sm), (blist, blist_sm), (ends, ends_sm), (rlist, rlist_sm)))
    ]
    for cp in to_sm:
        cp.start()

    for v in range(NVAR):
        for dc in (1, 3, 2, 0):
            for db in OFFS:
                s2[v, db, dc].wait_recv()
                if dc:
                    pass_on(v, 4 - db, dc)
    runs[RUN_ZERO] = jnp.zeros((BLK, BLK), BF16)
    gt[0] = jnp.zeros((BLK, BLK), BF16)
    for cp in to_sm:
        cp.wait()
    for v in range(NVAR):
        for b in (0, 3, 1, 2):
            for dc in OFFS:
                s3[v, b, dc].wait_recv()
    w_cp.wait()

    def forward_unit(u, acc):
        r, q = lax.div(u, 16), lax.rem(u, 16) * FC
        left, right = [], []
        for i in range(FC):
            left.append(w[flist_sm[r, q + i]])
            for v in range(NVAR):
                right.append(x[v][flist_sm[(v + 1) * 8 + r, q + i]])
        got = jnp.dot(
            jnp.concatenate(left, axis=1), jnp.concatenate(right, axis=0), preferred_element_type=F32
        )
        acc = jnp.where(flist_sm[32 + r, q] > 0, 0.0, acc) + got
        runs[u] = acc.astype(BF16)
        return acc

    lax.fori_loop(0, FU, forward_unit, jnp.zeros((BLK, BLK), F32), unroll=2)

    half = NB // 2
    mine, theirs = feat * half, (1 - feat) * half
    for i in range(half):
        send_a[i] = runs[ends_sm[2, theirs + i]]
    cp_a = send(send_a, full.at[feat], feat_s.at[0], feat_r.at[0], other)
    for i in range(half):
        full[feat, i] = runs[ends_sm[2, mine + i]]
    cp_a.wait_recv()

    wt[...] = jnp.zeros_like(wt)
    cp_g = []
    for i in range(half):
        left, right = full[0, i], full[1, i]
        pre = jnp.dot(left, weight[0:BLK, :], preferred_element_type=F32)
        pre += jnp.dot(right, weight[BLK:, :], preferred_element_type=F32)
        sig = jax.nn.sigmoid(pre)
        nodes = pl.ds(i * BLK, BLK)
        hidden[nodes, :] = (pre * sig).astype(BF16)
        grad = (cot[nodes, :].astype(F32) * (sig * (1.0 + pre * (1.0 - sig)))).astype(BF16)
        send_g[i] = lax.dot_general(
            weight[pl.ds((1 - feat) * BLK, BLK), :], grad, (((1,), (1,)), ((), ())), preferred_element_type=F32
        ).astype(BF16)
        cp = send(send_g.at[i], gt.at[1 + mine + i], feat_s.at[1 + i], feat_r.at[1 + i], other)
        cp_g.append(cp)
        gt[1 + mine + i] = lax.dot_general(
            weight[pl.ds(feat * BLK, BLK), :], grad, (((1,), (1,)), ((), ())), preferred_element_type=F32
        ).astype(BF16)
        for h, part in ((0, left), (1, right)):
            wt[h] += lax.dot_general(part, grad, (((0,), (0,)), ((), ())), preferred_element_type=F32)
    cp_w = send(wt.at[1 - feat], wt_in, feat_s.at[7], feat_r.at[7], other)
    for cp in cp_g:
        cp.wait_recv()

    def backward_unit(u, acc):
        r, q = lax.div(u, 64), lax.rem(u, 64) * BC
        left = [gt[blist_sm[8 + r, q + i]] for i in range(BC)]
        right = [w[blist_sm[r, q + i]] for i in range(BC)]
        got = jnp.dot(
            jnp.concatenate(left, axis=1), jnp.concatenate(right, axis=0), preferred_element_type=F32
        )
        acc = jnp.where(blist_sm[16 + r, q] > 0, 0.0, acc) + got
        runs[u] = acc.astype(BF16)
        return acc

    lax.fori_loop(0, BU, backward_unit, jnp.zeros((BLK, BLK), F32), unroll=6)

    packed = list(s2.values())
    for cp in packed:
        cp.wait_send()
    b3, b2, b1 = {}, {}, {}

    def fill(v, g, b):
        for d in range(4):
            t = turn[v]
            z = lax.rem(cz + jnp.where(t == 0, d, jnp.where(t == 1, g, b)), 4)
            xx = lax.rem(cx + jnp.where(t == 0, b, jnp.where(t == 1, d, g)), 4)
            yy = lax.rem(cy + jnp.where(t == 0, g, jnp.where(t == 1, b, d)), 4)
            slot = NB + (z * 16 + xx * 4 + yy) * 2
            for k in range(2):
                s = slot + k
                run = ends_sm[lax.div(s, BLK), lax.rem(s, BLK)]
                y[v][(g * 4 + b) * 8 + d * 2 + k] = runs[run, pl.ds(FIRST[v], ROWS[v])]

    def go_back(v, lam, kap):
        src = y[v].at[pl.ds(lam * 8, 8)] if kap == 0 else y[v].at[pl.ds(Y_ONE + ((kap - 1) * 4 + lam) * 8, 8)]
        i = (v * 4 + lam) * 4 + kap
        b2[v, lam, kap] = send(
            src, y[v].at[pl.ds(Y_TWO + ((4 - lam - 1) * 4 + kap) * 8, 8)],
            b2_s.at[i], b2_r.at[i], peer(v, 1, lam),
        )

    for b in (1, 3, 2, 0):
        for v in range(NVAR):
            for g in OFFS:
                fill(v, g, b)
                i = (v * 4 + g) * 4 + b
                b3[v, g, b] = send(
                    y[v].at[pl.ds((g * 4 + b) * 8, 8)],
                    y[v].at[pl.ds(Y_ONE + ((4 - g - 1) * 4 + b) * 8, 8)],
                    b3_s.at[i], b3_r.at[i], peer(v, 2, g),
                )
            fill(v, 0, b)
            if b:
                go_back(v, b, 0)

    cp_w.wait_recv()
    wt[feat] = wt[feat] + wt_in[...]
    gz, gx, gy = [], [], []

    def gw_copy(store, n, src, dst, axis, off):
        cp = send(src, dst, gw_s.at[n], gw_r.at[n], (moved(axis == 0, axis == 1, off), feat))
        store.append(cp)

    for off in OFFS:
        to = lax.rem(cz + off, 4)
        gw_copy(gz, off, wt.at[feat, pl.ds(to * 32, 32)], gw0.at[off], 0, off)

    for b in (1, 3, 2):
        for v in range(NVAR):
            for g in OFFS:
                b3[v, g, b].wait_recv()
                go_back(v, b, 4 - g)
        if b == 1:
            for cp in gz:
                cp.wait_recv()
            gw0[0] = wt[feat, pl.ds(cz * 32, 32)] + gw0[1] + gw0[2] + gw0[3]
            for off in OFFS:
                to = lax.rem(cx + off, 4)
                gw_copy(gx, 4 + off, gw0.at[0, pl.ds(to * 8, 8)], gw1.at[off], 1, off)
        if b == 3:
            for cp in gx:
                cp.wait_recv()
            gw2[cy] = gw0[0, pl.ds(cx * 8, 8)] + gw1[1] + gw1[2] + gw1[3]
            for off in OFFS:
                gw_copy(gy, 8 + off, gw2.at[cy], gw2.at[cy], 2, off)
    for cp in gy:
        cp.wait_recv()
    scale = float(64 * NB * BLK) ** (-0.5)
    gx2, gz2 = [], []
    gw3[cz, pl.ds(cx * 8, 8)] = (gw2[0] + gw2[1] + gw2[2] + gw2[3]) * scale
    for off in OFFS:
        gw_copy(gx2, 12 + off, gw3.at[cz, pl.ds(cx * 8, 8)], gw3.at[cz, pl.ds(cx * 8, 8)], 1, off)

    runs_r = runs

    for v in range(NVAR):
        for g in OFFS:
            b3[v, g, 0].wait_recv()
    for v in range(NVAR):
        n = ROWS[v]
        for lam in OFFS:
            for kap in range(4):
                b2[v, lam, kap].wait_recv()
        for o in (1, 3, 2, 0):
            r = (v * 4 + o) * 2

            def add(q, acc, v=v, r=r):
                code = rlist_sm[r, q]
                acc = jnp.where(code >= 512, 0.0, acc) + y[v][jnp.minimum(code & 511, Y_SIZE - 1)].astype(F32)
                rr[v][q] = acc.astype(BF16)
                return acc

            lax.fori_loop(0, 32, add, jnp.zeros((n, BLK), F32), unroll=4)
            rr[v][32] = jnp.zeros((n, BLK), BF16)
            for j in range(NB):
                ag[v][o * NB + j] = rr[v][rlist_sm[r + 1, j]]
            if o:
                i = v * 4 + o
                b1[v, o] = send(
                    ag[v].at[pl.ds(o * NB, NB)], vin[v].at[pl.ds((4 - o - 1) * NB, NB)],
                    b1_s.at[i], b1_r.at[i], peer(v, 0, o),
                )

    for cp in gx2:
        cp.wait_recv()
    for off in OFFS:
        gw_copy(gz2, off + 16, gw3.at[cz], gw3.at[cz], 0, off)

    for v in range(NVAR):
        for off in OFFS:
            b1[v, off].wait_recv()
    for j in range(NB):
        run = ends_sm[0, j]
        parts = []
        for v in range(NVAR):
            total = runs[run, pl.ds(FIRST[v], ROWS[v])].astype(F32) + ag[v][j].astype(F32)
            for off in range(3):
                total += vin[v][off * NB + j].astype(F32)
            parts.append(total)
        grad_out[pl.ds(j * BLK, BLK), :] = jnp.transpose(jnp.concatenate(parts, axis=0)).astype(BF16)

    for cp in gz2:
        cp.wait_recv()
    for z in range(4):
        gw_out[pl.ds(z * 32, 32), :] = gw3[z]

    for cp in started:
        if not any(cp is p for p in packed):
            cp.wait_send()


def local(features, tile_weights, tile_rows, tile_slots, send_blocks, weight, cotangent):
    dma = lambda n: pltpu.SemaphoreType.DMA((n,))
    vmem = lambda *shape, dtype=BF16: pltpu.VMEM(shape, dtype)
    smem = lambda *shape: pltpu.SMEM(shape, I32)
    in_vmem = pl.BlockSpec(memory_space=pltpu.VMEM)
    table = send_blocks.reshape(1, BLK)
    nodes = NB * BLK
    scratch = [
        vmem(TILES, BLK, BLK),
        *[vmem(X_SIZE, n, BLK) for n in ROWS],
        *[vmem(Y_SIZE, n, BLK) for n in ROWS],
        *[vmem(4 * NB, n, BLK) for n in ROWS],
        *[vmem(3 * NB, n, BLK) for n in ROWS],
        *[vmem(33, n, BLK) for n in ROWS],
        vmem(BU + 1, BLK, BLK),
        vmem(12, 1, BLK, dtype=I32), smem(12, 1, BLK),
        vmem(40, BLK, dtype=I32), smem(40, BLK),
        vmem(24, BLK, dtype=I32), smem(24, BLK),
        vmem(8, BLK, dtype=I32), smem(8, BLK),
        vmem(24, BLK, dtype=I32), smem(24, BLK),
        vmem(2, NB // 2, BLK, BLK), vmem(NB // 2, BLK, BLK), vmem(NB + 1, BLK, BLK), vmem(NB // 2, BLK, BLK),
        vmem(2, BLK, 256, dtype=F32), vmem(BLK, 256, dtype=F32),
        vmem(4, 32, 256, dtype=F32), vmem(4, 8, 256, dtype=F32), vmem(4, 8, 256, dtype=F32),
        vmem(4, 32, 256, dtype=F32),
        dma(1), dma(5), dma(8), dma(8), dma(12), dma(12),
        dma(12), dma(12), dma(48), dma(48), dma(48), dma(48),
        dma(48), dma(48), dma(48), dma(48), dma(12), dma(12), dma(20), dma(20),
    ]
    return pl.pallas_call(
        body,
        out_shape=(
            jax.ShapeDtypeStruct((nodes // 2, 256), BF16),
            jax.ShapeDtypeStruct((nodes, BLK), BF16),
            jax.ShapeDtypeStruct((BLK, 256), F32),
        ),
        in_specs=[
            in_vmem, pl.BlockSpec(memory_space=pl.ANY), in_vmem, in_vmem, in_vmem,
            pl.BlockSpec(memory_space=pltpu.SMEM), in_vmem, in_vmem,
        ],
        out_specs=(in_vmem, in_vmem, in_vmem),
        scratch_shapes=scratch,
        compiler_params=pltpu.CompilerParams(
            collective_id=0, has_side_effects=True, vmem_limit_bytes=64 * 2**20 - 2**16
        ),
        cost_estimate=pl.CostEstimate(flops=6 * 10**9, bytes_accessed=24 * 2**20, transcendentals=400000),
    )(
        features.reshape(NB, BLK, BLK), tile_weights, tile_rows.reshape(5, BLK), tile_slots.reshape(5, BLK),
        table, table, weight, cotangent,
    )


def solution(mesh):
    placed = (
        P("dom", "feat"),
        P("dom", None, None),
        P("dom"),
        P("dom"),
        P("dom", None, None),
        P(),
        P(("dom", "feat"), None),
    )
    return jax.shard_map(
        local,
        mesh=mesh,
        in_specs=placed,
        out_specs=(P(("dom", "feat"), None), P("dom", "feat"), P("feat", None)),
        check_vma=False,
    )
```

time: 539 us -> 145 us (0.27); the launches traced: 532 us -> 145 us
  waiting for transfers between devices: 211 us -> 0 us
  matrix products: 149 us -> 0 us
  Pallas kernels: 0 us -> 138 us
  local copies, waits for them, and re-layouts: 126 us -> 6.52 us
  starting transfers between devices: 20.4 us -> 0 us
  between operations: 14.4 us -> 0.64 us
  blocking collectives: 8.26 us -> 0 us
    dot_general x11 -> x0, matrix products: 149 us -> none  [the longest x3 52.1 us: exact_dot(): jnp.dot(selector, values, preferred_element_type=jnp.float32, precision=l...]
    psum x1 -> x0, waiting for transfers between devices: 145 us -> none  [local(): grad_weight = lax.psum(weight_part, 'dom') * factor]
    pallas_call x0 -> x1, Pallas kernels: none -> 138 us  [local(): pl.pallas_call(body, out_shape=(jax.ShapeDtypeStruct((nodes // 2, 256), B...]
    dot_general x2 -> x0, local copies, waits for them, and re-layouts: 88 us -> none  [the longest x1 44 us: local(): jnp.einsum('tij,tjf->tif', tile_weights, picked, preferred_element_type=j...]
    all_to_all x2 -> x0, waiting for transfers between devices: 52.5 us -> none  [the longest x1 52.5 us: local(): lax.all_to_all(outgoing, 'dom', split_axis=0, concat_axis=0, tiled=True)]
    all_to_all x2 -> x0, starting transfers between devices: 20.3 us -> none  [the longest x1 12.2 us: local(): lax.all_to_all(outgoing, 'dom', split_axis=0, concat_axis=0, tiled=True)]
    reduce_scatter x1 -> x0, waiting for transfers between devices: 14.3 us -> none  [local(): lax.psum_scatter(weight_term, 'feat', scatter_dimension=0, tiled=True)]
    reshape x3 -> x1, local copies, waits for them, and re-layouts: 13.3 us -> 0.65 us  [local(): table = send_blocks.reshape(1, BLK)]
  transfers between devices with their start and end apart: 4 -> 0, of which waited for: 3 -> 0; matrix products, arithmetic and copies ran while one was open for 1% -> 0% of each run, Pallas kernels for 0% -> 0%
where the time goes in v1:
time: 145 us
  Pallas kernels  138 us (95%)
  local copies, waits for them, and re-layouts  6.52 us (4%)
    pallas_call x1, Pallas kernels, local(): pl.pallas_call(body, out_shape=(jax.ShapeDtypeStruct((nodes // 2, 256), B...  138 us
    unnamed x4, local copies, waits for them, and re-layouts  5.87 us

profile of v1, /device:TPU:2, one launch (start us, length us, event | category | flops | bytes accessed | tf_op | source)
XLA Modules:
  0.0 145.1 jit_solution(11991262149712094487)
XLA Ops:
  0.6 0.8 copy.11
  1.4 0.7 reshape.21.tab_ref.tab_sm
  2.1 137.9 %shard_map.94 = (bf16[768,256]{1,0:T(8,128)(2,1)}, bf16[1536,128]{1,0:T(8,128)(2,1)}, f32[128,256]{1,0:T(8,128)}) custom-call(bf16[12,128,128]{2,1,0:T(8,128)(2,1)} %bitcast.3, bf16[640,128,128]{2,1,0:T(8,128)(2,1)} %tiles_hbm.1, s32[5,128]{1,0:T(8,128)} %bitcast.4, s32[5,128]{1,0:T(8,128)} %bitcast.5, s32[1,128]{1,0:T(1,128)} %reshape.21.tab_ref.tab_sm, ...), custom_call_target="tpu_custom_call" | custom-call | flops 6000000000 | bytes 25165824 | tf_op jit(solution)/shard_map/pallas_call | solution.py:524
  140.0 1.8 %copy.15 = bf16[768,256]{1,0:T(8,128)(2,1)} copy(bf16[768,256]{1,0:T(8,128)(2,1)} %get-tuple-element.6) | data formatting | bytes 786432
  141.8 1.8 %copy.16 = bf16[1536,128]{1,0:T(8,128)(2,1)} copy(bf16[1536,128]{1,0:T(8,128)(2,1)} %get-tuple-element.7) | data formatting | bytes 786432
  143.5 1.6 %copy.17 = f32[128,256]{1,0:T(8,128)} copy(f32[128,256]{1,0:T(8,128)} %get-tuple-element.8) | data formatting | bytes 262144

commit v2 on v1

--- a/solution.py
+++ b/solution.py
@@ -19,7 +19,7 @@
 FIRST = (0, 48, 96)
 
 FC, BC = 8, 2
-FU = 92
+FU = 96
 BU = 390
 FCH, BCH = 6, 7
 
@@ -30,12 +30,12 @@
 
 
 def body(
-    feats, tiles_hbm, rows_ref, slots_ref, tab_ref, tab_sm, weight, cot,
-    hidden, grad_out, gw_out,
+    feats, tiles_hbm, rows_ref, slots_ref, tab_in, weight_hbm, cot_hbm,
+    hidden_hbm, grad_out, gw_out,
     w, x0, x1, x2, y0, y1, y2, ag0, ag1, ag2, v0, v1, v2, rr0, rr1, rr2,
     runs, tabs, tabs_sm, flist, flist_sm, blist, blist_sm, ends, ends_sm, rlist, rlist_sm,
-    full, send_a, gt, send_g, wt, wt_in, gw0, gw1, gw2, gw3,
-    w_sem, sm_sem, feat_s, feat_r, tab_s, tab_r,
+    weight, cot, hidden, tab_ref, full, send_a, gt, send_g, wt, wt_in, gw0, gw1, gw2, gw3,
+    in_sem, sm_sem, feat_s, feat_r, tab_s, tab_r,
     s1_s, s1_r, s2_s, s2_r, s3_s, s3_r, b3_s, b3_r, b2_s, b2_r, b1_s, b1_r, gw_s, gw_r,
 ):
     x, y, ag, vin, rr = (x0, x1, x2), (y0, y1, y2), (ag0, ag1, ag2), (v0, v1, v2), (rr0, rr1, rr2)
@@ -65,15 +65,15 @@
         yy = lax.rem(cy + jnp.where(t == 0, dc, jnp.where(t == 1, db, 0)), 4)
         return z * 16 + xx * 4 + yy
 
-    started = []
-
     def send(src, dst, ssem, rsem, device):
         cp = pltpu.make_async_remote_copy(
             src_ref=src, dst_ref=dst, send_sem=ssem, recv_sem=rsem, device_id=device, device_id_type=MESH
         )
         cp.start()
-        started.append(cp)
         return cp
+
+    def await_arrival(ref, sem):
+        pltpu.make_async_copy(ref, ref, sem).wait()
 
     other = (dom, 1 - feat)
 
@@ -86,20 +86,22 @@
     pl.semaphore_signal(barrier, inc=1, device_id=other, device_id_type=MESH)
     pl.semaphore_wait(barrier, 10)
 
-    tab_cp, s1, s2, s3 = {}, {}, {}, {}
+    tab_ref[...] = jnp.concatenate([tab_in[0:1, :], tab_in[1:2, :]], axis=1)
     for v in range(NVAR):
         for off in OFFS:
-            i = v * 4 + off
-            tab_cp[v, off] = send(tab_ref, tabs.at[v * 4 + (4 - off)], tab_s.at[i], tab_r.at[i], peer(v, 0, off))
+            send(tab_ref, tabs.at[v * 4 + (4 - off)], tab_s.at[0], tab_r.at[0], peer(v, 0, off))
     for off in OFFS:
         for v in range(NVAR):
-            i = v * 4 + off
-            s1[v, off] = send(
+            send(
                 feats.at[:, pl.ds(FIRST[v], ROWS[v])], ag[v].at[pl.ds((4 - off) * NB, NB)],
-                s1_s.at[i], s1_r.at[i], peer(v, 0, off),
+                s1_s.at[v], s1_r.at[v], peer(v, 0, off),
             )
-    w_cp = pltpu.make_async_copy(tiles_hbm, w, w_sem.at[0])
-    w_cp.start()
+    loads = [
+        pltpu.make_async_copy(a, b, in_sem.at[i])
+        for i, (a, b) in enumerate(((weight_hbm, weight), (cot_hbm, cot), (tiles_hbm, w)))
+    ]
+    for cp in loads:
+        cp.start()
 
     for v in range(NVAR):
         chunk = pl.ds(FIRST[v], ROWS[v])
@@ -150,7 +152,7 @@
         far = jnp.maximum(slot - NB, 0)
         k = far & 1
         d, b, g = roles(v, digits(lax.shift_right_logical(far, 1)))
-        near = X_HOP + ((b * 4) * 4 + d) * 2 + k
+        near = X_HOP + b * 8 + d * 2 + k
         end = X_END + (((g - 1) * 4 + b) * 4 + d) * 2 + k
         return jnp.where(slot < NB, X_OWN + slot, jnp.where(g == 0, near, end))
 
@@ -186,42 +188,37 @@
         )
         flist[pl.ds(32 + q, 1), :] = starts
 
-    for v in range(NVAR):
-        for off in OFFS:
-            tab_cp[v, off].wait_recv()
+    await_arrival(tabs.at[pl.ds(0, 9)], tab_r.at[0])
     tabs_cp = pltpu.make_async_copy(tabs, tabs_sm, sm_sem.at[0])
     tabs_cp.start()
     tabs_cp.wait()
 
     def pack(v, db, dc, dst, base):
-        at = reader(v, db, dc) * 2
+        at = reader(v, db, dc)
         for d in range(4):
             for k in range(2):
-                j = tabs_sm[v * 4 + d, 0, at + k]
+                j = tabs_sm[v * 4 + d, 0, at + k * 64]
                 dst[base + d * 2 + k] = ag[v][d * NB + j]
 
     def pass_on(v, b, dc):
-        i = (v * 4 + b) * 4 + dc
-        s3[v, b, dc] = send(
-            x[v].at[pl.ds(X_HOP + (b * 4 + dc) * 8, 8)],
+        send(
+            x[v].at[pl.ds(X_HOP + (dc * 4 + b) * 8, 8)],
             x[v].at[pl.ds(X_END + ((4 - dc - 1) * 4 + b) * 8, 8)],
-            s3_s.at[i], s3_r.at[i], peer(v, 2, dc),
-        )
-
-    for v in range(NVAR):
-        for off in OFFS:
-            s1[v, off].wait_recv()
+            s3_s.at[v], s3_r.at[v], peer(v, 2, dc),
+        )
+
+    for v in range(NVAR):
+        await_arrival(ag[v].at[pl.ds(NB, 3 * NB)], s1_r.at[v])
         for dc in (1, 3, 2, 0):
-            pack(v, 0, dc, x[v], X_HOP + dc * 8)
+            pack(v, 0, dc, x[v], X_HOP + dc * 32)
             if dc:
                 pass_on(v, 0, dc)
             for db in OFFS:
                 base = (db * 4 + dc) * 8
                 pack(v, db, dc, y[v], base)
-                i = (v * 4 + db) * 4 + dc
-                s2[v, db, dc] = send(
-                    y[v].at[pl.ds(base, 8)], x[v].at[pl.ds(X_HOP + ((4 - db) * 4 + dc) * 8, 8)],
-                    s2_s.at[i], s2_r.at[i], peer(v, 1, db),
+                send(
+                    y[v].at[pl.ds(base, 8)], x[v].at[pl.ds(X_HOP + (dc * 4 + (4 - db)) * 8, 8)],
+                    s2_s.at[v], s2_r.at[v * 4 + dc], peer(v, 1, db),
                 )
 
     slot_c = [column(s) for s in slot_r]
@@ -254,10 +251,10 @@
 
     index1 = lax.broadcasted_iota(I32, (1, BLK), 1)
     for v in range(NVAR):
-        k = index1 & 1
-        d, b, g = roles(v, digits(lax.shift_right_logical(index1, 1)))
+        k = lax.shift_right_logical(index1, 6)
+        d, b, g = roles(v, digits(index1 & 63))
         own = Y_TWO + ((b - 1) * 4 + g) * 8 + k
-        loc = jnp.where(b > 0, own, jnp.where(g > 0, Y_ONE + (g - 1) * 32 + k, k))
+        loc = jnp.where(b > 0, own, jnp.where(g > 0, Y_ONE + (g - 1) * 8 + k, k))
         loc_c = column(loc)
         for o in range(4):
             block = jnp.where(d == 0, tabs[v * 4 + o], 64)
@@ -282,19 +279,17 @@
 
     for v in range(NVAR):
         for dc in (1, 3, 2, 0):
-            for db in OFFS:
-                s2[v, db, dc].wait_recv()
-                if dc:
-                    pass_on(v, 4 - db, dc)
+            await_arrival(x[v].at[pl.ds(X_HOP + (dc * 4 + 1) * 8, 24)], s2_r.at[v * 4 + dc])
+            if dc:
+                for b in (1, 3, 2):
+                    pass_on(v, b, dc)
     runs[RUN_ZERO] = jnp.zeros((BLK, BLK), BF16)
     gt[0] = jnp.zeros((BLK, BLK), BF16)
     for cp in to_sm:
         cp.wait()
     for v in range(NVAR):
-        for b in (0, 3, 1, 2):
-            for dc in OFFS:
-                s3[v, b, dc].wait_recv()
-    w_cp.wait()
+        await_arrival(x[v].at[pl.ds(X_END, 96)], s3_r.at[v])
+    loads[2].wait()
 
     def forward_unit(u, acc):
         r, q = lax.div(u, 16), lax.rem(u, 16) * FC
@@ -310,19 +305,20 @@
         runs[u] = acc.astype(BF16)
         return acc
 
-    lax.fori_loop(0, FU, forward_unit, jnp.zeros((BLK, BLK), F32), unroll=2)
+    lax.fori_loop(0, FU, forward_unit, jnp.zeros((BLK, BLK), F32), unroll=16)
 
     half = NB // 2
     mine, theirs = feat * half, (1 - feat) * half
     for i in range(half):
         send_a[i] = runs[ends_sm[2, theirs + i]]
-    cp_a = send(send_a, full.at[feat], feat_s.at[0], feat_r.at[0], other)
+    send(send_a, full.at[feat], feat_s.at[0], feat_r.at[0], other)
+    for cp in loads[:2]:
+        cp.wait()
     for i in range(half):
         full[feat, i] = runs[ends_sm[2, mine + i]]
-    cp_a.wait_recv()
+    await_arrival(full.at[1 - feat], feat_r.at[0])
 
     wt[...] = jnp.zeros_like(wt)
-    cp_g = []
     for i in range(half):
         left, right = full[0, i], full[1, i]
         pre = jnp.dot(left, weight[0:BLK, :], preferred_element_type=F32)
@@ -334,16 +330,16 @@
         send_g[i] = lax.dot_general(
             weight[pl.ds((1 - feat) * BLK, BLK), :], grad, (((1,), (1,)), ((), ())), preferred_element_type=F32
         ).astype(BF16)
-        cp = send(send_g.at[i], gt.at[1 + mine + i], feat_s.at[1 + i], feat_r.at[1 + i], other)
-        cp_g.append(cp)
+        send(send_g.at[i], gt.at[1 + mine + i], feat_s.at[1], feat_r.at[1], other)
         gt[1 + mine + i] = lax.dot_general(
             weight[pl.ds(feat * BLK, BLK), :], grad, (((1,), (1,)), ((), ())), preferred_element_type=F32
         ).astype(BF16)
         for h, part in ((0, left), (1, right)):
             wt[h] += lax.dot_general(part, grad, (((0,), (0,)), ((), ())), preferred_element_type=F32)
-    cp_w = send(wt.at[1 - feat], wt_in, feat_s.at[7], feat_r.at[7], other)
-    for cp in cp_g:
-        cp.wait_recv()
+    send(wt.at[1 - feat], wt_in, feat_s.at[2], feat_r.at[2], other)
+    hidden_cp = pltpu.make_async_copy(hidden, hidden_hbm, in_sem.at[0])
+    hidden_cp.start()
+    await_arrival(gt.at[pl.ds(1 + theirs, half)], feat_r.at[1])
 
     def backward_unit(u, acc):
         r, q = lax.div(u, 64), lax.rem(u, 64) * BC
@@ -356,12 +352,10 @@
         runs[u] = acc.astype(BF16)
         return acc
 
-    lax.fori_loop(0, BU, backward_unit, jnp.zeros((BLK, BLK), F32), unroll=6)
-
-    packed = list(s2.values())
-    for cp in packed:
-        cp.wait_send()
-    b3, b2, b1 = {}, {}, {}
+    lax.fori_loop(0, BU, backward_unit, jnp.zeros((BLK, BLK), F32), unroll=39)
+
+    for v in range(NVAR):
+        await_arrival(y[v].at[pl.ds(32, 96)], s2_s.at[v])
 
     def fill(v, g, b):
         for d in range(4):
@@ -376,75 +370,62 @@
                 y[v][(g * 4 + b) * 8 + d * 2 + k] = runs[run, pl.ds(FIRST[v], ROWS[v])]
 
     def go_back(v, lam, kap):
-        src = y[v].at[pl.ds(lam * 8, 8)] if kap == 0 else y[v].at[pl.ds(Y_ONE + ((kap - 1) * 4 + lam) * 8, 8)]
-        i = (v * 4 + lam) * 4 + kap
-        b2[v, lam, kap] = send(
+        src = y[v].at[pl.ds(lam * 8, 8)] if kap == 0 else y[v].at[pl.ds(Y_ONE + (lam * 3 + kap - 1) * 8, 8)]
+        send(
             src, y[v].at[pl.ds(Y_TWO + ((4 - lam - 1) * 4 + kap) * 8, 8)],
-            b2_s.at[i], b2_r.at[i], peer(v, 1, lam),
+            b2_s.at[v], b2_r.at[v], peer(v, 1, lam),
         )
 
     for b in (1, 3, 2, 0):
         for v in range(NVAR):
             for g in OFFS:
                 fill(v, g, b)
-                i = (v * 4 + g) * 4 + b
-                b3[v, g, b] = send(
+                send(
                     y[v].at[pl.ds((g * 4 + b) * 8, 8)],
-                    y[v].at[pl.ds(Y_ONE + ((4 - g - 1) * 4 + b) * 8, 8)],
-                    b3_s.at[i], b3_r.at[i], peer(v, 2, g),
+                    y[v].at[pl.ds(Y_ONE + (b * 3 + (4 - g - 1)) * 8, 8)],
+                    b3_s.at[v], b3_r.at[v * 4 + b], peer(v, 2, g),
                 )
             fill(v, 0, b)
             if b:
                 go_back(v, b, 0)
 
-    cp_w.wait_recv()
+    await_arrival(wt_in, feat_r.at[2])
     wt[feat] = wt[feat] + wt_in[...]
-    gz, gx, gy = [], [], []
-
-    def gw_copy(store, n, src, dst, axis, off):
-        cp = send(src, dst, gw_s.at[n], gw_r.at[n], (moved(axis == 0, axis == 1, off), feat))
-        store.append(cp)
+
+    def gw_copy(n, src, dst, axis, off):
+        send(src, dst, gw_s.at[n], gw_r.at[n], (moved(axis == 0, axis == 1, off), feat))
 
     for off in OFFS:
         to = lax.rem(cz + off, 4)
-        gw_copy(gz, off, wt.at[feat, pl.ds(to * 32, 32)], gw0.at[off], 0, off)
+        gw_copy(0, wt.at[feat, pl.ds(to * 32, 32)], gw0.at[off], 0, off)
 
     for b in (1, 3, 2):
         for v in range(NVAR):
-            for g in OFFS:
-                b3[v, g, b].wait_recv()
-                go_back(v, b, 4 - g)
+            await_arrival(y[v].at[pl.ds(Y_ONE + b * 24, 24)], b3_r.at[v * 4 + b])
+            for kap in (3, 1, 2):
+                go_back(v, b, kap)
         if b == 1:
-            for cp in gz:
-                cp.wait_recv()
+            await_arrival(gw0.at[pl.ds(1, 3)], gw_r.at[0])
             gw0[0] = wt[feat, pl.ds(cz * 32, 32)] + gw0[1] + gw0[2] + gw0[3]
             for off in OFFS:
                 to = lax.rem(cx + off, 4)
-                gw_copy(gx, 4 + off, gw0.at[0, pl.ds(to * 8, 8)], gw1.at[off], 1, off)
+                gw_copy(1, gw0.at[0, pl.ds(to * 8, 8)], gw1.at[off], 1, off)
         if b == 3:
-            for cp in gx:
-                cp.wait_recv()
+            await_arrival(gw1.at[pl.ds(1, 3)], gw_r.at[1])
             gw2[cy] = gw0[0, pl.ds(cx * 8, 8)] + gw1[1] + gw1[2] + gw1[3]
             for off in OFFS:
-                gw_copy(gy, 8 + off, gw2.at[cy], gw2.at[cy], 2, off)
-    for cp in gy:
-        cp.wait_recv()
+                gw_copy(2, gw2.at[cy], gw2.at[cy], 2, off)
+    await_arrival(gw1.at[pl.ds(1, 3)], gw_r.at[2])
     scale = float(64 * NB * BLK) ** (-0.5)
-    gx2, gz2 = [], []
     gw3[cz, pl.ds(cx * 8, 8)] = (gw2[0] + gw2[1] + gw2[2] + gw2[3]) * scale
     for off in OFFS:
-        gw_copy(gx2, 12 + off, gw3.at[cz, pl.ds(cx * 8, 8)], gw3.at[cz, pl.ds(cx * 8, 8)], 1, off)
-
-    runs_r = runs
-
-    for v in range(NVAR):
-        for g in OFFS:
-            b3[v, g, 0].wait_recv()
+        gw_copy(3, gw3.at[cz, pl.ds(cx * 8, 8)], gw3.at[cz, pl.ds(cx * 8, 8)], 1, off)
+
+    for v in range(NVAR):
+        await_arrival(y[v].at[pl.ds(Y_ONE, 24)], b3_r.at[v * 4])
     for v in range(NVAR):
         n = ROWS[v]
-        for lam in OFFS:
-            for kap in range(4):
-                b2[v, lam, kap].wait_recv()
+        await_arrival(y[v].at[pl.ds(Y_TWO, 96)], b2_r.at[v])
         for o in (1, 3, 2, 0):
             r = (v * 4 + o) * 2
 
@@ -459,20 +440,17 @@
             for j in range(NB):
                 ag[v][o * NB + j] = rr[v][rlist_sm[r + 1, j]]
             if o:
-                i = v * 4 + o
-                b1[v, o] = send(
+                send(
                     ag[v].at[pl.ds(o * NB, NB)], vin[v].at[pl.ds((4 - o - 1) * NB, NB)],
-                    b1_s.at[i], b1_r.at[i], peer(v, 0, o),
+                    b1_s.at[v], b1_r.at[v], peer(v, 0, o),
                 )
 
-    for cp in gx2:
-        cp.wait_recv()
+    await_arrival(gw1.at[pl.ds(1, 3)], gw_r.at[3])
     for off in OFFS:
-        gw_copy(gz2, off + 16, gw3.at[cz], gw3.at[cz], 0, off)
-
-    for v in range(NVAR):
-        for off in OFFS:
-            b1[v, off].wait_recv()
+        gw_copy(4, gw3.at[cz], gw3.at[cz], 0, off)
+
+    for v in range(NVAR):
+        await_arrival(vin[v], b1_r.at[v])
     for j in range(NB):
         run = ends_sm[0, j]
         parts = []
@@ -483,14 +461,37 @@
             parts.append(total)
         grad_out[pl.ds(j * BLK, BLK), :] = jnp.transpose(jnp.concatenate(parts, axis=0)).astype(BF16)
 
-    for cp in gz2:
-        cp.wait_recv()
+    await_arrival(gw0.at[pl.ds(1, 3)], gw_r.at[4])
     for z in range(4):
         gw_out[pl.ds(z * 32, 32), :] = gw3[z]
 
-    for cp in started:
-        if not any(cp is p for p in packed):
-            cp.wait_send()
+    hidden_cp.wait()
+    await_arrival(tabs.at[pl.ds(0, 9)], tab_s.at[0])
+    await_arrival(send_a, feat_s.at[0])
+    await_arrival(send_g, feat_s.at[1])
+    await_arrival(wt_in, feat_s.at[2])
+    for v in range(NVAR):
+        await_arrival(ag[v].at[pl.ds(NB, 3 * NB)], s1_s.at[v])
+        await_arrival(x[v].at[pl.ds(X_HOP + 32, 96)], s3_s.at[v])
+        await_arrival(y[v].at[pl.ds(32, 96)], b3_s.at[v])
+        await_arrival(y[v].at[pl.ds(Y_TWO, 96)], b2_s.at[v])
+        await_arrival(ag[v].at[pl.ds(NB, 3 * NB)], b1_s.at[v])
+    for n, ref in enumerate((gw0, gw1, gw1, gw1, gw0)):
+        await_arrival(ref.at[pl.ds(1, 3)], gw_s.at[n])
+
+
+def hand_over(*refs):
+    n = (len(refs) - 1) // 3
+    sem = refs[-1]
+    inward = [pltpu.make_async_copy(refs[i], refs[2 * n + i], sem.at[i]) for i in range(n)]
+    outward = [pltpu.make_async_copy(refs[2 * n + i], refs[n + i], sem.at[n + i]) for i in range(n)]
+    for cp in inward:
+        cp.start()
+    for a, b in zip(inward, outward):
+        a.wait()
+        b.start()
+    for cp in outward:
+        cp.wait()
 
 
 def local(features, tile_weights, tile_rows, tile_slots, send_blocks, weight, cotangent):
@@ -498,7 +499,7 @@
     vmem = lambda *shape, dtype=BF16: pltpu.VMEM(shape, dtype)
     smem = lambda *shape: pltpu.SMEM(shape, I32)
     in_vmem = pl.BlockSpec(memory_space=pltpu.VMEM)
-    table = send_blocks.reshape(1, BLK)
+    anywhere = pl.BlockSpec(memory_space=pl.ANY)
     nodes = NB * BLK
     scratch = [
         vmem(TILES, BLK, BLK),
@@ -513,26 +514,25 @@
         vmem(24, BLK, dtype=I32), smem(24, BLK),
         vmem(8, BLK, dtype=I32), smem(8, BLK),
         vmem(24, BLK, dtype=I32), smem(24, BLK),
+        vmem(256, 256), vmem(nodes // 2, 256), vmem(nodes // 2, 256), vmem(1, BLK, dtype=I32),
         vmem(2, NB // 2, BLK, BLK), vmem(NB // 2, BLK, BLK), vmem(NB + 1, BLK, BLK), vmem(NB // 2, BLK, BLK),
         vmem(2, BLK, 256, dtype=F32), vmem(BLK, 256, dtype=F32),
         vmem(4, 32, 256, dtype=F32), vmem(4, 8, 256, dtype=F32), vmem(4, 8, 256, dtype=F32),
         vmem(4, 32, 256, dtype=F32),
-        dma(1), dma(5), dma(8), dma(8), dma(12), dma(12),
-        dma(12), dma(12), dma(48), dma(48), dma(48), dma(48),
-        dma(48), dma(48), dma(48), dma(48), dma(12), dma(12), dma(20), dma(20),
+        dma(3), dma(5), dma(3), dma(3), dma(1), dma(1),
+        dma(3), dma(3), dma(3), dma(12), dma(3), dma(3),
+        dma(3), dma(12), dma(3), dma(3), dma(3), dma(3), dma(5), dma(5),
     ]
-    return pl.pallas_call(
+    out_shape = (
+        jax.ShapeDtypeStruct((nodes // 2, 256), BF16),
+        jax.ShapeDtypeStruct((nodes, BLK), BF16),
+        jax.ShapeDtypeStruct((BLK, 256), F32),
+    )
+    results = pl.pallas_call(
         body,
-        out_shape=(
-            jax.ShapeDtypeStruct((nodes // 2, 256), BF16),
-            jax.ShapeDtypeStruct((nodes, BLK), BF16),
-            jax.ShapeDtypeStruct((BLK, 256), F32),
-        ),
-        in_specs=[
-            in_vmem, pl.BlockSpec(memory_space=pl.ANY), in_vmem, in_vmem, in_vmem,
-            pl.BlockSpec(memory_space=pltpu.SMEM), in_vmem, in_vmem,
-        ],
-        out_specs=(in_vmem, in_vmem, in_vmem),
+        out_shape=out_shape,
+        in_specs=[in_vmem, anywhere, in_vmem, in_vmem, in_vmem, anywhere, anywhere],
+        out_specs=(anywhere, in_vmem, in_vmem),
         scratch_shapes=scratch,
         compiler_params=pltpu.CompilerParams(
             collective_id=0, has_side_effects=True, vmem_limit_bytes=64 * 2**20 - 2**16
@@ -540,8 +540,15 @@
         cost_estimate=pl.CostEstimate(flops=6 * 10**9, bytes_accessed=24 * 2**20, transcendentals=400000),
     )(
         features.reshape(NB, BLK, BLK), tile_weights, tile_rows.reshape(5, BLK), tile_slots.reshape(5, BLK),
-        table, table, weight, cotangent,
+        jnp.swapaxes(send_blocks, 1, 2).reshape(2, 64), weight, cotangent,
     )
+    return pl.pallas_call(
+        hand_over,
+        out_shape=out_shape,
+        in_specs=[anywhere] * 3,
+        out_specs=(anywhere,) * 3,
+        scratch_shapes=[*[pltpu.VMEM(o.shape, o.dtype) for o in out_shape], dma(6)],
+    )(*results)
 
 
 def solution(mesh):

time: 145 us -> 122 us (0.84)
  Pallas kernels: 138 us -> 121 us
  local copies, waits for them, and re-layouts: 6.52 us -> 0 us
    pallas_call x1 -> x2, Pallas kernels: 138 us -> 121 us  [the longest x1 119 us: local(): pl.pallas_call(body, out_shape=out_shape, in_specs=[in_vmem, anywhere, in...]
    unnamed x4 -> x0, local copies, waits for them, and re-layouts: 5.87 us -> none
where the time goes in v2:
time: 122 us
  Pallas kernels  121 us (99%)
    pallas_call x1, Pallas kernels, local(): pl.pallas_call(body, out_shape=out_shape, in_specs=[in_vmem, anywhere, in...  119 us

profile of v2, /device:TPU:2, one launch (start us, length us, event | category | flops | bytes accessed | tf_op | source)
XLA Modules:
  0.0 121.9 jit_solution(8295543785537587548)
XLA Ops:
  0.6 119.2 %shard_map.94 = (bf16[768,256]{1,0:T(8,128)(2,1)}, bf16[1536,128]{1,0:T(8,128)(2,1)}, f32[128,256]{1,0:T(8,128)}) custom-call(bf16[12,128,128]{2,1,0:T(8,128)(2,1)} %bitcast.6, bf16[640,128,128]{2,1,0:T(8,128)(2,1)} %tiles_hbm.1, s32[5,128]{1,0:T(8,128)} %bitcast.7, s32[5,128]{1,0:T(8,128)} %bitcast.8, s32[2,64]{1,0:T(2,128)} %bitcast.9, ...), custom_call_target="tpu_custom_call" | custom-call | flops 6000000000 | bytes 25165824 | tf_op jit(solution)/shard_map/pallas_call | solution.py:531
  119.8 2.0 %shard_map.95 = (bf16[768,256]{1,0:T(8,128)(2,1)}, bf16[1536,128]{1,0:T(8,128)(2,1)}, f32[128,256]{1,0:T(8,128)}) custom-call(bf16[768,256]{1,0:T(8,128)(2,1)} %get-tuple-element.6.refs_0_, bf16[1536,128]{1,0:T(8,128)(2,1)} %get-tuple-element.7.refs_1_, f32[128,256]{1,0:T(8,128)} %get-tuple-element.8.refs_2_), custom_call_target="tpu_custom_call" | custom-call | tf_op jit(solution)/shard_map/pallas_call | solution.py:545

commit v3 on v2

--- a/solution.py
+++ b/solution.py
@@ -33,8 +33,8 @@
     feats, tiles_hbm, rows_ref, slots_ref, tab_in, weight_hbm, cot_hbm,
     hidden_hbm, grad_out, gw_out,
     w, x0, x1, x2, y0, y1, y2, ag0, ag1, ag2, v0, v1, v2, rr0, rr1, rr2,
-    runs, tabs, tabs_sm, flist, flist_sm, blist, blist_sm, ends, ends_sm, rlist, rlist_sm,
-    weight, cot, hidden, tab_ref, full, send_a, gt, send_g, wt, wt_in, gw0, gw1, gw2, gw3,
+    runs, tabs, tabs_sm, own_sm, flist, flist_sm, blist, blist_sm, ends, ends_sm, rlist, rlist_sm,
+    weight, cot, hidden, grads, tab_ref, full, send_a, gt, send_g, wt, wt_in, gw0, gw1, gw2, gw3,
     in_sem, sm_sem, feat_s, feat_r, tab_s, tab_r,
     s1_s, s1_r, s2_s, s2_r, s3_s, s3_r, b3_s, b3_r, b2_s, b2_r, b1_s, b1_r, gw_s, gw_r,
 ):
@@ -87,6 +87,8 @@
     pl.semaphore_wait(barrier, 10)
 
     tab_ref[...] = jnp.concatenate([tab_in[0:1, :], tab_in[1:2, :]], axis=1)
+    own_cp = pltpu.make_async_copy(tab_ref, own_sm, sm_sem.at[5])
+    own_cp.start()
     for v in range(NVAR):
         for off in OFFS:
             send(tab_ref, tabs.at[v * 4 + (4 - off)], tab_s.at[0], tab_r.at[0], peer(v, 0, off))
@@ -112,6 +114,22 @@
             ag[v][j] = block
         tabs[v * 4] = tab_ref[...]
 
+    def hop(v, db, dc, begin, n):
+        send(
+            y[v].at[pl.ds((db * 4 + dc) * 8 + begin, n)],
+            x[v].at[pl.ds(X_HOP + (dc * 4 + (4 - db)) * 8 + begin, n)],
+            s2_s.at[v], s2_r.at[v * 4 + dc], peer(v, 1, db),
+        )
+
+    own_cp.wait()
+    for v in range(NVAR):
+        for dc in (1, 3, 2, 0):
+            for db in OFFS:
+                at = reader(v, db, dc)
+                for k in range(2):
+                    y[v][(db * 4 + dc) * 8 + k] = feats[own_sm[0, at + k * 64], pl.ds(FIRST[v], ROWS[v])]
+                hop(v, db, dc, 0, 2)
+
     lane = lax.broadcasted_iota(I32, (BLK, BLK), 1)
     sub = lax.broadcasted_iota(I32, (BLK, BLK), 0)
     ones = jnp.ones((BLK, BLK), I32)
@@ -195,7 +213,7 @@
 
     def pack(v, db, dc, dst, base):
         at = reader(v, db, dc)
-        for d in range(4):
+        for d in range(1 if db else 0, 4):
             for k in range(2):
                 j = tabs_sm[v * 4 + d, 0, at + k * 64]
                 dst[base + d * 2 + k] = ag[v][d * NB + j]
@@ -216,10 +234,7 @@
             for db in OFFS:
                 base = (db * 4 + dc) * 8
                 pack(v, db, dc, y[v], base)
-                send(
-                    y[v].at[pl.ds(base, 8)], x[v].at[pl.ds(X_HOP + (dc * 4 + (4 - db)) * 8, 8)],
-                    s2_s.at[v], s2_r.at[v * 4 + dc], peer(v, 1, db),
-                )
+                hop(v, db, dc, 2, 6)
 
     slot_c = [column(s) for s in slot_r]
     counts = [sum(jnp.sum(hits(s == lane + h * BLK), axis=0, keepdims=True) for s in slot_c) for h in range(2)]
@@ -278,16 +293,16 @@
         cp.start()
 
     for v in range(NVAR):
-        for dc in (1, 3, 2, 0):
+        for dc in OFFS:
             await_arrival(x[v].at[pl.ds(X_HOP + (dc * 4 + 1) * 8, 24)], s2_r.at[v * 4 + dc])
-            if dc:
-                for b in (1, 3, 2):
-                    pass_on(v, b, dc)
+            for b in (1, 3, 2):
+                pass_on(v, b, dc)
     runs[RUN_ZERO] = jnp.zeros((BLK, BLK), BF16)
     gt[0] = jnp.zeros((BLK, BLK), BF16)
     for cp in to_sm:
         cp.wait()
     for v in range(NVAR):
+        await_arrival(x[v].at[pl.ds(X_HOP + 8, 24)], s2_r.at[v * 4])
         await_arrival(x[v].at[pl.ds(X_END, 96)], s3_r.at[v])
     loads[2].wait()
 
@@ -307,7 +322,7 @@
 
     lax.fori_loop(0, FU, forward_unit, jnp.zeros((BLK, BLK), F32), unroll=16)
 
-    half = NB // 2
+    half, nodes_here = NB // 2, NB // 2 * BLK
     mine, theirs = feat * half, (1 - feat) * half
     for i in range(half):
         send_a[i] = runs[ends_sm[2, theirs + i]]
@@ -318,7 +333,6 @@
         full[feat, i] = runs[ends_sm[2, mine + i]]
     await_arrival(full.at[1 - feat], feat_r.at[0])
 
-    wt[...] = jnp.zeros_like(wt)
     for i in range(half):
         left, right = full[0, i], full[1, i]
         pre = jnp.dot(left, weight[0:BLK, :], preferred_element_type=F32)
@@ -327,6 +341,7 @@
         nodes = pl.ds(i * BLK, BLK)
         hidden[nodes, :] = (pre * sig).astype(BF16)
         grad = (cot[nodes, :].astype(F32) * (sig * (1.0 + pre * (1.0 - sig)))).astype(BF16)
+        grads[nodes, :] = grad
         send_g[i] = lax.dot_general(
             weight[pl.ds((1 - feat) * BLK, BLK), :], grad, (((1,), (1,)), ((), ())), preferred_element_type=F32
         ).astype(BF16)
@@ -334,9 +349,6 @@
         gt[1 + mine + i] = lax.dot_general(
             weight[pl.ds(feat * BLK, BLK), :], grad, (((1,), (1,)), ((), ())), preferred_element_type=F32
         ).astype(BF16)
-        for h, part in ((0, left), (1, right)):
-            wt[h] += lax.dot_general(part, grad, (((0,), (0,)), ((), ())), preferred_element_type=F32)
-    send(wt.at[1 - feat], wt_in, feat_s.at[2], feat_r.at[2], other)
     hidden_cp = pltpu.make_async_copy(hidden, hidden_hbm, in_sem.at[0])
     hidden_cp.start()
     await_arrival(gt.at[pl.ds(1 + theirs, half)], feat_r.at[1])
@@ -376,8 +388,8 @@
             b2_s.at[v], b2_r.at[v], peer(v, 1, lam),
         )
 
-    for b in (1, 3, 2, 0):
-        for v in range(NVAR):
+    for v in range(NVAR):
+        for b in (1, 3, 2, 0):
             for g in OFFS:
                 fill(v, g, b)
                 send(
@@ -389,42 +401,51 @@
             if b:
                 go_back(v, b, 0)
 
-    await_arrival(wt_in, feat_r.at[2])
-    wt[feat] = wt[feat] + wt_in[...]
+    for h in range(2):
+        part = full[h].reshape(nodes_here, BLK)
+        wt[h] = lax.dot_general(part, grads[...], (((0,), (0,)), ((), ())), preferred_element_type=F32)
+    send(wt.at[1 - feat], wt_in, feat_s.at[2], feat_r.at[2], other)
 
     def gw_copy(n, src, dst, axis, off):
         send(src, dst, gw_s.at[n], gw_r.at[n], (moved(axis == 0, axis == 1, off), feat))
 
-    for off in OFFS:
-        to = lax.rem(cz + off, 4)
-        gw_copy(0, wt.at[feat, pl.ds(to * 32, 32)], gw0.at[off], 0, off)
-
-    for b in (1, 3, 2):
-        for v in range(NVAR):
-            await_arrival(y[v].at[pl.ds(Y_ONE + b * 24, 24)], b3_r.at[v * 4 + b])
-            for kap in (3, 1, 2):
-                go_back(v, b, kap)
-        if b == 1:
+    def gw_step(n):
+        if n == 0:
+            await_arrival(wt_in, feat_r.at[2])
+            wt[feat] = wt[feat] + wt_in[...]
+            for off in OFFS:
+                gw_copy(0, wt.at[feat, pl.ds(lax.rem(cz + off, 4) * 32, 32)], gw0.at[off], 0, off)
+        elif n == 1:
             await_arrival(gw0.at[pl.ds(1, 3)], gw_r.at[0])
             gw0[0] = wt[feat, pl.ds(cz * 32, 32)] + gw0[1] + gw0[2] + gw0[3]
             for off in OFFS:
-                to = lax.rem(cx + off, 4)
-                gw_copy(1, gw0.at[0, pl.ds(to * 8, 8)], gw1.at[off], 1, off)
-        if b == 3:
+                gw_copy(1, gw0.at[0, pl.ds(lax.rem(cx + off, 4) * 8, 8)], gw1.at[off], 1, off)
+        elif n == 2:
             await_arrival(gw1.at[pl.ds(1, 3)], gw_r.at[1])
             gw2[cy] = gw0[0, pl.ds(cx * 8, 8)] + gw1[1] + gw1[2] + gw1[3]
             for off in OFFS:
                 gw_copy(2, gw2.at[cy], gw2.at[cy], 2, off)
-    await_arrival(gw1.at[pl.ds(1, 3)], gw_r.at[2])
-    scale = float(64 * NB * BLK) ** (-0.5)
-    gw3[cz, pl.ds(cx * 8, 8)] = (gw2[0] + gw2[1] + gw2[2] + gw2[3]) * scale
-    for off in OFFS:
-        gw_copy(3, gw3.at[cz, pl.ds(cx * 8, 8)], gw3.at[cz, pl.ds(cx * 8, 8)], 1, off)
-
-    for v in range(NVAR):
+        elif n == 3:
+            await_arrival(gw1.at[pl.ds(1, 3)], gw_r.at[2])
+            scale = float(64 * NB * BLK) ** (-0.5)
+            gw3[cz, pl.ds(cx * 8, 8)] = (gw2[0] + gw2[1] + gw2[2] + gw2[3]) * scale
+            for off in OFFS:
+                gw_copy(3, gw3.at[cz, pl.ds(cx * 8, 8)], gw3.at[cz, pl.ds(cx * 8, 8)], 1, off)
+        else:
+            await_arrival(gw1.at[pl.ds(1, 3)], gw_r.at[3])
+            for off in OFFS:
+                gw_copy(4, gw3.at[cz], gw3.at[cz], 0, off)
+
+    for v in range(NVAR):
+        for b in (1, 3, 2):
+            await_arrival(y[v].at[pl.ds(Y_ONE + b * 24, 24)], b3_r.at[v * 4 + b])
+            for kap in (3, 1, 2):
+                go_back(v, b, kap)
+        gw_step(v)
+
+    for v in range(NVAR):
+        n = ROWS[v]
         await_arrival(y[v].at[pl.ds(Y_ONE, 24)], b3_r.at[v * 4])
-    for v in range(NVAR):
-        n = ROWS[v]
         await_arrival(y[v].at[pl.ds(Y_TWO, 96)], b2_r.at[v])
         for o in (1, 3, 2, 0):
             r = (v * 4 + o) * 2
@@ -444,10 +465,8 @@
                     ag[v].at[pl.ds(o * NB, NB)], vin[v].at[pl.ds((4 - o - 1) * NB, NB)],
                     b1_s.at[v], b1_r.at[v], peer(v, 0, o),
                 )
-
-    await_arrival(gw1.at[pl.ds(1, 3)], gw_r.at[3])
-    for off in OFFS:
-        gw_copy(4, gw3.at[cz], gw3.at[cz], 0, off)
+        if v < 2:
+            gw_step(3 + v)
 
     for v in range(NVAR):
         await_arrival(vin[v], b1_r.at[v])
@@ -509,17 +528,17 @@
         *[vmem(3 * NB, n, BLK) for n in ROWS],
         *[vmem(33, n, BLK) for n in ROWS],
         vmem(BU + 1, BLK, BLK),
-        vmem(12, 1, BLK, dtype=I32), smem(12, 1, BLK),
+        vmem(12, 1, BLK, dtype=I32), smem(12, 1, BLK), smem(1, BLK),
         vmem(40, BLK, dtype=I32), smem(40, BLK),
         vmem(24, BLK, dtype=I32), smem(24, BLK),
         vmem(8, BLK, dtype=I32), smem(8, BLK),
         vmem(24, BLK, dtype=I32), smem(24, BLK),
-        vmem(256, 256), vmem(nodes // 2, 256), vmem(nodes // 2, 256), vmem(1, BLK, dtype=I32),
+        vmem(256, 256), vmem(nodes // 2, 256), vmem(nodes // 2, 256), vmem(nodes // 2, 256), vmem(1, BLK, dtype=I32),
         vmem(2, NB // 2, BLK, BLK), vmem(NB // 2, BLK, BLK), vmem(NB + 1, BLK, BLK), vmem(NB // 2, BLK, BLK),
         vmem(2, BLK, 256, dtype=F32), vmem(BLK, 256, dtype=F32),
         vmem(4, 32, 256, dtype=F32), vmem(4, 8, 256, dtype=F32), vmem(4, 8, 256, dtype=F32),
         vmem(4, 32, 256, dtype=F32),
-        dma(3), dma(5), dma(3), dma(3), dma(1), dma(1),
+        dma(3), dma(6), dma(3), dma(3), dma(1), dma(1),
         dma(3), dma(3), dma(3), dma(12), dma(3), dma(3),
         dma(3), dma(12), dma(3), dma(3), dma(3), dma(3), dma(5), dma(5),
     ]

time: 122 us -> 117 us (0.959); the launches traced: 122 us -> 116 us
  Pallas kernels: 121 us -> 115 us
    pallas_call x1, Pallas kernels: 119 us -> 113 us  [local(): pl.pallas_call(body, out_shape=out_shape, in_specs=[in_vmem, anywhere, in...]
where the time goes in v3:
time: 117 us; the launch traced here: 116 us
  Pallas kernels  115 us (98%)
    pallas_call x1, Pallas kernels, local(): pl.pallas_call(body, out_shape=out_shape, in_specs=[in_vmem, anywhere, in...  113 us

profile of v3, /device:TPU:2, one launch (start us, length us, event | category | flops | bytes accessed | tf_op | source)
XLA Modules:
  0.0 115.6 jit_solution(15881411345695579905)
XLA Ops:
  0.6 112.8 %shard_map.94 = (bf16[768,256]{1,0:T(8,128)(2,1)}, bf16[1536,128]{1,0:T(8,128)(2,1)}, f32[128,256]{1,0:T(8,128)}) custom-call(bf16[12,128,128]{2,1,0:T(8,128)(2,1)} %bitcast.6, bf16[640,128,128]{2,1,0:T(8,128)(2,1)} %tiles_hbm.1, s32[5,128]{1,0:T(8,128)} %bitcast.7, s32[5,128]{1,0:T(8,128)} %bitcast.8, s32[2,64]{1,0:T(2,128)} %bitcast.9, ...), custom_call_target="tpu_custom_call" | custom-call | flops 6000000000 | bytes 25165824 | tf_op jit(solution)/shard_map/pallas_call | solution.py:550
  113.5 2.0 %shard_map.95 = (bf16[768,256]{1,0:T(8,128)(2,1)}, bf16[1536,128]{1,0:T(8,128)(2,1)}, f32[128,256]{1,0:T(8,128)}) custom-call(bf16[768,256]{1,0:T(8,128)(2,1)} %get-tuple-element.6.refs_0_, bf16[1536,128]{1,0:T(8,128)(2,1)} %get-tuple-element.7.refs_1_, f32[128,256]{1,0:T(8,128)} %get-tuple-element.8.refs_2_), custom_call_target="tpu_custom_call" | custom-call | tf_op jit(solution)/shard_map/pallas_call | solution.py:564

commit v4 on v3

--- a/solution.py
+++ b/solution.py
@@ -30,11 +30,11 @@
 
 
 def body(
-    feats, tiles_hbm, rows_ref, slots_ref, tab_in, weight_hbm, cot_hbm,
+    feats_hbm, tiles_hbm, rows_hbm, slots_hbm, tab_hbm, weight_hbm, cot_hbm,
     hidden_hbm, grad_out, gw_out,
     w, x0, x1, x2, y0, y1, y2, ag0, ag1, ag2, v0, v1, v2, rr0, rr1, rr2,
     runs, tabs, tabs_sm, own_sm, flist, flist_sm, blist, blist_sm, ends, ends_sm, rlist, rlist_sm,
-    weight, cot, hidden, grads, tab_ref, full, send_a, gt, send_g, wt, wt_in, gw0, gw1, gw2, gw3,
+    weight, cot, hidden, grads, feats, rows_ref, slots_ref, tab_in, tab_ref, full, send_a, gt, send_g, wt, wt_in, gw0, gw1, gw2, gw3,
     in_sem, sm_sem, feat_s, feat_r, tab_s, tab_r,
     s1_s, s1_r, s2_s, s2_r, s3_s, s3_r, b3_s, b3_r, b2_s, b2_r, b1_s, b1_r, gw_s, gw_r,
 ):
@@ -84,6 +84,16 @@
                 barrier, inc=1, device_id=(moved(axis == 0, axis == 1, off), feat), device_id_type=MESH
             )
     pl.semaphore_signal(barrier, inc=1, device_id=other, device_id_type=MESH)
+    first = [
+        pltpu.make_async_copy(a, b, in_sem.at[3 + i])
+        for i, (a, b) in enumerate(
+            ((tab_hbm, tab_in), (feats_hbm, feats), (rows_hbm, rows_ref), (slots_hbm, slots_ref))
+        )
+    ]
+    for cp in first:
+        cp.start()
+    for cp in first:
+        cp.wait()
     pl.semaphore_wait(barrier, 10)
 
     tab_ref[...] = jnp.concatenate([tab_in[0:1, :], tab_in[1:2, :]], axis=1)
@@ -333,22 +343,28 @@
         full[feat, i] = runs[ends_sm[2, mine + i]]
     await_arrival(full.at[1 - feat], feat_r.at[0])
 
-    for i in range(half):
-        left, right = full[0, i], full[1, i]
+    span = 3
+    for i in range(0, half, span):
+        nodes = pl.ds(i * BLK, span * BLK)
+        left, right = (full[h, pl.ds(i, span)].reshape(span * BLK, BLK) for h in range(2))
         pre = jnp.dot(left, weight[0:BLK, :], preferred_element_type=F32)
         pre += jnp.dot(right, weight[BLK:, :], preferred_element_type=F32)
         sig = jax.nn.sigmoid(pre)
-        nodes = pl.ds(i * BLK, BLK)
         hidden[nodes, :] = (pre * sig).astype(BF16)
         grad = (cot[nodes, :].astype(F32) * (sig * (1.0 + pre * (1.0 - sig)))).astype(BF16)
         grads[nodes, :] = grad
-        send_g[i] = lax.dot_general(
-            weight[pl.ds((1 - feat) * BLK, BLK), :], grad, (((1,), (1,)), ((), ())), preferred_element_type=F32
-        ).astype(BF16)
-        send(send_g.at[i], gt.at[1 + mine + i], feat_s.at[1], feat_r.at[1], other)
-        gt[1 + mine + i] = lax.dot_general(
-            weight[pl.ds(feat * BLK, BLK), :], grad, (((1,), (1,)), ((), ())), preferred_element_type=F32
-        ).astype(BF16)
+        for here in (False, True):
+            rows = weight[pl.ds((feat if here else 1 - feat) * BLK, BLK), :]
+            cols = lax.dot_general(rows, grad, (((1,), (1,)), ((), ())), preferred_element_type=F32).astype(BF16)
+            for t in range(span):
+                block = cols[:, t * BLK : (t + 1) * BLK]
+                if here:
+                    gt[1 + mine + i + t] = block
+                else:
+                    send_g[i + t] = block
+            if not here:
+                blocks = pl.ds(i, span)
+                send(send_g.at[blocks], gt.at[pl.ds(1 + mine + i, span)], feat_s.at[1], feat_r.at[1], other)
     hidden_cp = pltpu.make_async_copy(hidden, hidden_hbm, in_sem.at[0])
     hidden_cp.start()
     await_arrival(gt.at[pl.ds(1 + theirs, half)], feat_r.at[1])
@@ -533,12 +549,13 @@
         vmem(24, BLK, dtype=I32), smem(24, BLK),
         vmem(8, BLK, dtype=I32), smem(8, BLK),
         vmem(24, BLK, dtype=I32), smem(24, BLK),
-        vmem(256, 256), vmem(nodes // 2, 256), vmem(nodes // 2, 256), vmem(nodes // 2, 256), vmem(1, BLK, dtype=I32),
+        vmem(256, 256), vmem(nodes // 2, 256), vmem(nodes // 2, 256), vmem(nodes // 2, 256),
+        vmem(NB, BLK, BLK), vmem(5, BLK, dtype=I32), vmem(5, BLK, dtype=I32), vmem(2, 64, dtype=I32), vmem(1, BLK, dtype=I32),
         vmem(2, NB // 2, BLK, BLK), vmem(NB // 2, BLK, BLK), vmem(NB + 1, BLK, BLK), vmem(NB // 2, BLK, BLK),
         vmem(2, BLK, 256, dtype=F32), vmem(BLK, 256, dtype=F32),
         vmem(4, 32, 256, dtype=F32), vmem(4, 8, 256, dtype=F32), vmem(4, 8, 256, dtype=F32),
         vmem(4, 32, 256, dtype=F32),
-        dma(3), dma(6), dma(3), dma(3), dma(1), dma(1),
+        dma(7), dma(6), dma(3), dma(3), dma(1), dma(1),
         dma(3), dma(3), dma(3), dma(12), dma(3), dma(3),
         dma(3), dma(12), dma(3), dma(3), dma(3), dma(3), dma(5), dma(5),
     ]
@@ -550,7 +567,7 @@
     results = pl.pallas_call(
         body,
         out_shape=out_shape,
-        in_specs=[in_vmem, anywhere, in_vmem, in_vmem, in_vmem, anywhere, anywhere],
+        in_specs=[anywhere] * 7,
         out_specs=(anywhere, in_vmem, in_vmem),
         scratch_shapes=scratch,
         compiler_params=pltpu.CompilerParams(

time: 117 us -> 115 us (0.983)
  Pallas kernels: 115 us -> 113 us
    pallas_call x1, Pallas kernels: 113 us -> 111 us  [local(): pl.pallas_call(body, out_shape=out_shape, in_specs=[anywhere] * 7, out_sp...]
where the time goes in v4:
time: 115 us; the launch traced here: 114 us
  Pallas kernels  113 us (98%)
    pallas_call x1, Pallas kernels, local(): pl.pallas_call(body, out_shape=out_shape, in_specs=[anywhere] * 7, out_sp...  111 us

profile of v4, /device:TPU:2, one launch (start us, length us, event | category | flops | bytes accessed | tf_op | source)
XLA Modules:
  0.0 113.6 jit_solution(9582876432718430465)
XLA Ops:
  0.6 110.8 %shard_map.94 = (bf16[768,256]{1,0:T(8,128)(2,1)}, bf16[1536,128]{1,0:T(8,128)(2,1)}, f32[128,256]{1,0:T(8,128)}) custom-call(bf16[12,128,128]{2,1,0:T(8,128)(2,1)} %bitcast.6, bf16[640,128,128]{2,1,0:T(8,128)(2,1)} %tiles_hbm.1, s32[5,128]{1,0:T(8,128)} %bitcast.7, s32[5,128]{1,0:T(8,128)} %bitcast.8, s32[2,64]{1,0:T(2,128)} %bitcast.9, ...), custom_call_target="tpu_custom_call" | custom-call | flops 6000000000 | bytes 25165824 | tf_op jit(solution)/shard_map/pallas_call | solution.py:567
  111.5 2.0 %shard_map.95 = (bf16[768,256]{1,0:T(8,128)(2,1)}, bf16[1536,128]{1,0:T(8,128)(2,1)}, f32[128,256]{1,0:T(8,128)}) custom-call(bf16[768,256]{1,0:T(8,128)(2,1)} %get-tuple-element.6.refs_0_, bf16[1536,128]{1,0:T(8,128)(2,1)} %get-tuple-element.7.refs_1_, f32[128,256]{1,0:T(8,128)} %get-tuple-element.8.refs_2_), custom_call_target="tpu_custom_call" | custom-call | tf_op jit(solution)/shard_map/pallas_call | solution.py:581
